TPU v7x, 256 devices: a whole 4x4x8 slice. The times are simulated.
256 devices in a mesh: occ: 64 (over z, x, y_hi), vir: 4 (over y_lo, core).
Axes of the slice: x: 4, y: 4 (y_hi: 2, y_lo: 2; y = y_hi * 2 + y_lo), z: 8, core: 2. Of those that a mesh axis runs over, the one named last changes fastest.
Arguments:
- amplitudes: bfloat16 [64, 384, 64, 384], P('occ', 'vir'), may hold values from -6 to 6
- aux_ints: bfloat16 [384, 64, 1024], P('vir', None, 'occ'), may hold values from -0.109375 to 0.109375
- occ_irrep: int32 [64], replicated, may hold values from 0 to 7, as said below
- vir_irrep: int32 [384], replicated, may hold values from 0 to 7, as said below
Outputs:
- residual: bfloat16 [64, 384, 64, 384], P('occ', 'vir')
Inputs may be any that keep to these rules, and one draw needn't show every extreme that they name: `occ_irrep`: labels of the eight D2h irreps (a product of orbitals is totally symmetric when the XOR of their labels is 0); orbitals are ordered by irrep, labels never fall, and each irrep holds a multiple of 8 orbitals, possibly none. `vir_irrep`: labels of the eight D2h irreps; orbitals are ordered by irrep, labels never fall, and each irrep holds a multiple of 24 orbitals, possibly none.
All inputs are finite; a program needn't handle non-finite values.
Results may differ from a plain program's by a relative error of at most 0.0066.
Values may be sent and summed in bfloat16 or wider, within the bound.
A program may use at most 128 MiB of HBM per device.

v0:
```python
import jax
import jax.numpy as jnp
from jax import lax
from jax.sharding import PartitionSpec as P


def on_device(amplitudes, aux_ints, occ_irrep, vir_irrep):
    row_count = amplitudes.shape[0]
    vir_block = amplitudes.shape[1]
    first_row = lax.axis_index("occ") * row_count
    first_vir = lax.axis_index("vir") * vir_block
    row_labels = lax.dynamic_slice_in_dim(occ_irrep, first_row, row_count)
    blk_labels = lax.dynamic_slice_in_dim(vir_irrep, first_vir, vir_block)
    labels = (
        row_labels[:, None, None, None]
        ^ blk_labels[None, :, None, None]
        ^ occ_irrep[None, None, :, None]
        ^ vir_irrep[None, None, None, :]
    )
    masked = jnp.where(labels == 0, amplitudes, jnp.zeros_like(amplitudes))
    moved = lax.all_to_all(masked, "vir", split_axis=3, concat_axis=1, tiled=True)
    swapped = jnp.transpose(moved, (0, 3, 2, 1))
    combined = (2.0 * masked.astype(jnp.float32) - swapped.astype(jnp.float32)).astype(jnp.bfloat16)
    gathered = lax.all_gather(aux_ints, "occ", axis=2, tiled=True)
    partial_value = jnp.einsum(
        "icka,ckp->iap", combined, gathered, preferred_element_type=jnp.float32
    )
    summed = lax.psum(partial_value, "vir")
    fitted = summed.astype(jnp.bfloat16)
    cycle_term = jnp.einsum(
        "bjp,iap->ibja", gathered, fitted, preferred_element_type=jnp.float32
    ).astype(jnp.bfloat16)
    received = lax.all_to_all(
        lax.all_to_all(cycle_term, "occ", split_axis=2, concat_axis=0, tiled=True),
        "vir",
        split_axis=3,
        concat_axis=1,
        tiled=True,
    )
    mirror = jnp.transpose(received, (2, 3, 0, 1))
    return (cycle_term.astype(jnp.float32) + mirror.astype(jnp.float32)).astype(jnp.bfloat16)


def solution(mesh):
    in_specs = (P("occ", "vir", None, None), P("vir", None, "occ"), P(), P())
    out_specs = P("occ", "vir", None, None)
    return jax.shard_map(
        on_device, mesh=mesh, in_specs=in_specs, out_specs=out_specs, check_vma=False
    )
```

profile of v0, /device:TPU:1, one launch (start us, length us, event | category | flops | bytes accessed | tf_op | source)
XLA Modules:
  0.0 547.3 jit_solution(1244695421669399425)
XLA Ops:
  6.5 0.0 copy-start.2
  6.5 0.0 copy-start.1
  6.5 0.0 all-gather.2.cloned.1.call-start
  6.5 0.7 all-gather.2.cloned.1.call-update
  7.3 9.5 %copy.16 = bf16[1,96,64,384]{1,2,0,3:T(8,128)(2,1)} copy(bf16[1,96,64,384]{3,2,1,0:T(8,128)(2,1)} %param.4) | data formatting | bytes 9437184 | tf_op args[0]
  16.7 0.0 copy-done.2
  16.7 0.6 dynamic_slice.6
  17.3 0.0 copy-done.1
  17.3 0.7 dynamic-slice_xor_fusion
  18.0 0.1 broadcast_xor_fusion
  18.1 4.8 fusion
  22.9 88.0 %all_to_all.36 = bf16[1,96,64,384]{1,2,0,3:T(8,128)(2,1)} all-to-all(bf16[1,96,64,384]{1,2,0,3:T(8,128)(2,1)S(1)} %fusion), channel_id=1, replica_groups=mesh['occ'=64,'vir'=4] {'vir'}, dimensions={3} | all-to-all | bytes 9437184 | tf_op jit(solution)/shard_map/all_to_all | solution.py:21
  110.9 15.1 %copy.17 = f32[1,96,64,4,96]{4,2,1,3,0:T(8,128)} copy(bf16[1,96,64,4,96]{1,2,4,3,0:T(8,128)(2,1)} %bitcast.43) | data formatting | bytes 14155776 | tf_op jit(solution)/shard_map/convert_element_type | solution.py:23
  126.0 11.3 %fusion.2 = bf16[96,64,384]{0,1,2:T(8,128)(2,1)} fusion(f32[1,96,64,384]{1,2,0,3:T(8,128)} %bitcast.41, bf16[1,96,64,384]{1,2,0,3:T(8,128)(2,1)} %copy.16, s32[384]{0:T(512)S(1)} %copy-done.1, s32[96,64]{0,1:T(8,128)S(1)} %broadcast_xor_fusion), kind=kLoop, calls=%fused_computation.6 | loop fusion | flops 16515072 | bytes 18900480 | tf_op jit(solution)/shard_map/reshape.5
  137.3 97.9 %all-gather.2.cloned.1.call-done = bf16[96,64,1024]{0,2,1:T(8,128)(2,1)} async-done(((bf16[96,64,16]{0,2,1:T(8,128)(2,1)}), bf16[96,64,1024]{0,2,1:T(8,128)(2,1)}) %all-gather.2.cloned.1.call-update) | async-done | bytes 12582928 | tf_op jit(solution)/shard_map/all_gather | solution.py:24
  235.2 18.3 %fusion.5 = f32[1,384,1024]{2,1,0:T(8,128)S(1)} fusion(bf16[96,64,1024]{0,2,1:T(8,128)(2,1)} %all-gather.2.cloned.1.call-done, bf16[96,64,384]{0,1,2:T(8,128)(2,1)} %fusion.2), kind=kOutput, calls=%fused_computation.10 | convolution fusion | flops 4831838208 | bytes 18874368 | tf_op jit(solution)/shard_map/icka,ckp->iap/dot_general | solution.py:25
  253.4 34.8 %all-reduce.1 = bf16[1,384,1024]{2,1,0:T(8,128)(2,1)S(1)} all-reduce(f32[1,384,1024]{2,1,0:T(8,128)S(1)} %fusion.5), channel_id=1, replica_groups=mesh['occ'=64,'vir'=4] {'vir'}, use_global_device_ids=true, to_apply=%region_0.1 | all-reduce | flops 393216 | bytes 2359296 | tf_op jit(solution)/shard_map/psum | solution.py:28
  288.3 10.9 %convolution_convert_fusion = bf16[384,96,64]{0,1,2:T(8,128)(2,1)S(1)} fusion(bf16[96,64,1024]{0,2,1:T(8,128)(2,1)} %all-gather.2.cloned.1.call-done, bf16[1,384,1024]{2,1,0:T(8,128)(2,1)S(1)} %all-reduce.1), kind=kOutput, calls=%fused_computation.9 | convolution fusion | flops 4834197504 | bytes 18087936 | tf_op jit(solution)/shard_map/bjp,iap->ibja/dot_general | solution.py:30
  299.2 0.0 copy-start
  299.2 2.2 copy-done
  301.4 113.8 %all_to_all.37 = bf16[1,96,64,384]{3,1,0,2:T(8,128)(2,1)} all-to-all(bf16[1,96,64,384]{3,1,0,2:T(8,128)(2,1)S(1)} %bitcast.45), channel_id=1, replica_groups=mesh['occ'=64,'vir'=4] {'occ'}, dimensions={2} | all-to-all | bytes 9437184 | tf_op jit(solution)/shard_map/all_to_all | solution.py:34
  415.2 8.7 %copy.20 = bf16[64,96,1,384]{1,0,2,3:T(8,128)(2,1)} copy(bf16[64,96,1,384]{3,1,0,2:T(8,128)(2,1)} %bitcast.46) | data formatting | bytes 9437184 | tf_op jit(solution)/shard_map/all_to_all | solution.py:34
  423.8 80.2 %all_to_all.38 = bf16[64,96,1,384]{1,0,2,3:T(8,128)(2,1)} all-to-all(bf16[64,96,1,384]{1,0,2,3:T(8,128)(2,1)} %copy.20), channel_id=1, replica_groups=mesh['occ'=64,'vir'=4] {'vir'}, dimensions={3} | all-to-all | bytes 9437184 | tf_op jit(solution)/shard_map/all_to_all | solution.py:33
  504.0 12.2 %copy.28 = f32[64,96,1,4,96]{1,3,4,0,2:T(4,128)} copy(bf16[64,96,1,4,96]{1,0,4,3,2:T(8,128)(2,1)} %bitcast.44) | data formatting | bytes 14155776 | tf_op jit(solution)/shard_map/convert_element_type | solution.py:41
  516.2 13.8 %reshape.71 = f32[64,384,1,96]{1,3,0,2:T(8,128)} reshape(f32[64,4,96,1,96]{2,1,4,0,3:T(4,128)} %bitcast.42) | data formatting | bytes 18874368 | tf_op jit(solution)/shard_map/convert_element_type | solution.py:41
  530.0 6.4 %fusion.1 = bf16[1,96,64,384]{3,1,2,0:T(8,128)(2,1)S(1)} fusion(f32[64,384,1,96]{1,3,0,2:T(8,128)} %reshape.71, bf16[384,96,64]{0,1,2:T(8,128)(2,1)} %copy-done), kind=kLoop, calls=%fused_computation.5 | loop fusion | flops 7077888 | bytes 18874368 | tf_op jit(solution)/shard_map/convert_element_type | solution.py:41
  536.5 4.0 copy.22
Async XLA Ops:
  6.5 10.2 %copy-start.2 = (s32[64]{0:T(128)S(1)}, s32[64]{0:T(128)}, u32[]{:S(2)}) copy-start(s32[64]{0:T(128)} %param.6) | copy-start | bytes 772
  6.5 10.8 %copy-start.1 = (s32[384]{0:T(512)S(1)}, s32[384]{0:T(512)}, u32[]{:S(2)}) copy-start(s32[384]{0:T(512)} %param.7) | copy-start | bytes 4612
  6.5 228.6 %all-gather.2.cloned.1.call-start = ((), (), s32[]{:S(2)}) async-start(), calls=%async_computation.3 | async-start | bytes 17039360 | tf_op jit(solution)/shard_map/all_gather | solution.py:24
  299.2 2.2 copy-start
Sparse Core Ops, SparseCore 0:
  10.8 224.3 all-gather.1
where the time goes:
time: 549 us; the launch traced here: 547 us
  blocking collectives  317 us (58%)
  waiting for transfers between devices  98.6 us (18%)
  local copies, waits for them, and re-layouts  66 us (12%)
  matrix products  29.1 us (5%)
  other arithmetic  23.4 us (4%)
  between operations  13.4 us (2%)
    all_to_all x1, blocking collectives, on_device(): lax.all_to_all(cycle_term, 'occ', split_axis=2, concat_axis=0, tiled=True)  114 us
    all_gather x1, waiting for transfers between devices, on_device(): gathered = lax.all_gather(aux_ints, 'occ', axis=2, tiled=True)  97.9 us
    all_to_all x1, blocking collectives, on_device(): lax.all_to_all(masked, 'vir', split_axis=3, concat_axis=1, tiled=True)  88 us
    all_to_all x1, blocking collectives, on_device(): lax.all_to_all(lax.all_to_all(cycle_term, 'occ', split_axis=2, concat_axi...  80.2 us
    psum x1, blocking collectives, on_device(): summed = lax.psum(partial_value, 'vir')  34.8 us
    convert_element_type x2, local copies, waits for them, and re-layouts, on_device(): mirror.astype(jnp.float32)  26 us
    dot_general x1, matrix products, on_device(): jnp.einsum('icka,ckp->iap', combined, gathered, preferred_element_type=jn...  18.3 us
    convert_element_type x1, local copies, waits for them, and re-layouts, on_device(): swapped.astype(jnp.float32)  15.1 us
  transfers between devices with their start and end apart: 1, of which 1 were waited for; matrix products, arithmetic and copies ran while one was open for 8% of the time, Pallas kernels for 0%

commit v1 on v0

v1 whole, which is shorter than its diff:
```python
import functools

import jax
import jax.numpy as jnp
from jax import lax
from jax.experimental import pallas as pl
from jax.experimental.pallas import tpu as pltpu
from jax.sharding import PartitionSpec as P

MESH = pl.DeviceIdType.MESH
NZ, NX, NY, NV = 8, 4, 2, 4
BF16, F32 = jnp.bfloat16, jnp.float32
GROUPS = ((0,), (1, 7), (2, 6), (3, 5), (4,))
COLUMNS = ((0,), (1, 3), (2,))
N_SEMS = 76


def position():
    o, v = lax.axis_index("occ"), lax.axis_index("vir")
    return o // (NX * NY), (o // NY) % NX, o % NY, v


def device(z, x, y, v):
    return ((z * NX + x) * NY + y, v)


def barrier(peers):
    sem = pltpu.get_barrier_semaphore()
    for peer in peers:
        pl.semaphore_signal(sem, 1, device_id=peer, device_id_type=MESH)
    pl.semaphore_wait(sem, len(peers))


def peers_of(z, x, y, v):
    ring = [
        device((z + 1) % NZ, x, y, v),
        device((z + NZ - 1) % NZ, x, y, v),
        device(z, (x + 1) % NX, y, v),
        device(z, (x + NX - 1) % NX, y, v),
        device(z, x, 1 - y, v),
    ]
    return ring + [device(z, x, y, (v + d) % NV) for d in range(1, NV)]


class Gather:
    def __init__(self, ref, rows, cut, send_sems, recv_sems):
        self.ref, self.rows, self.cut = ref, rows, cut
        self.width = ref.shape[1]
        self.send_sems, self.recv_sems = send_sems, recv_sems
        self.z, self.x, self.y, self.v = position()
        self.started = []

    def block(self, z, x, half):
        rows = self.rows
        if half is None:
            start, size = (z * NX + x) * NY * rows, NY * rows
        else:
            start, size = ((z * NX + x) * NY + half) * rows, rows
        return pl.ds(pl.multiple_of(start, 16), size)

    def copy(self, key, z, x, half, d):
        kind = key[0]
        index = {"az": 0, "ax": 8, "bx": 40, "bz": 44}[kind]
        if kind == "az":
            index += key[1] * 4 + key[2]
        elif kind == "ax":
            index += (key[1] * 8 + key[2]) * 2 + key[3]
        elif kind == "bx":
            index += key[1] * 2 + key[2]
        else:
            index += (key[1] * 4 + key[2]) * 4 + key[3]
        lanes = pl.ds(0, self.cut) if kind[0] == "a" else pl.ds(self.cut, self.width - self.cut)
        part = self.ref.at[self.block(z % NZ, x % NX, half), lanes]
        s = 1 - 2 * d
        if kind[1] == "z":
            target = device((self.z + s + NZ) % NZ, self.x, self.y, self.v)
        else:
            target = device(self.z, (self.x + s + NX) % NX, self.y, self.v)
        return pltpu.make_async_remote_copy(
            src_ref=part, dst_ref=part, send_sem=self.send_sems.at[index],
            recv_sem=self.recv_sems.at[index], device_id=target, device_id_type=MESH)

    def start(self, *args):
        copy = self.copy(*args)
        copy.start()
        self.started.append(args)

    def wait(self, *args):
        self.copy(*args).wait_recv()

    def az_send(self, d, t):
        s = 1 - 2 * d
        self.start(("az", d, t), self.z - s * t + NZ, self.x, d if t == 3 else None, d)

    def az_wait(self, d, t):
        s = 1 - 2 * d
        self.wait(("az", d, t), self.z - s * (t + 1) + NZ, self.x, d if t == 3 else None, d)

    def ax_send(self, d, delta, kind):
        s = 1 - 2 * d
        if kind == 0:
            self.start(("ax", d, delta, 0), self.z + delta, self.x, None, d)
        else:
            self.start(("ax", d, delta, 1), self.z + delta, self.x - s + NX, d, d)

    def ax_wait(self, d, delta, kind):
        s = 1 - 2 * d
        if kind == 0:
            self.wait(("ax", d, delta, 0), self.z + delta, self.x - s + NX, None, d)
        else:
            self.wait(("ax", d, delta, 1), self.z + delta, self.x - 2 * s + NX, d, d)

    def bx_send(self, d, kind):
        s = 1 - 2 * d
        if kind == 0:
            self.start(("bx", d, 0), self.z, self.x, None, d)
        else:
            self.start(("bx", d, 1), self.z, self.x - s + NX, d, d)

    def bx_wait(self, d, kind):
        s = 1 - 2 * d
        if kind == 0:
            self.wait(("bx", d, 0), self.z, self.x - s + NX, None, d)
        else:
            self.wait(("bx", d, 1), self.z, self.x - 2 * s + NX, d, d)

    def bz_send(self, d, xi, t):
        s = 1 - 2 * d
        self.start(("bz", d, xi, t), self.z - s * t + NZ, self.x + xi, d if t == 3 else None, d)

    def bz_wait(self, d, xi, t):
        s = 1 - 2 * d
        self.wait(("bz", d, xi, t), self.z - s * (t + 1) + NZ, self.x + xi, d if t == 3 else None, d)

    def wave(self, w):
        both = (0, 1)
        if w == 0:
            for d in both:
                self.az_send(d, 0)
                self.bx_send(d, 0)
            for d in both:
                self.ax_send(d, 0, 0)
                self.bz_send(d, 0, 0)
            return
        if w <= 4:
            for d in both:
                self.az_wait(d, w - 1)
                if w <= 3:
                    self.az_send(d, w)
            for delta in GROUPS[w]:
                for d in both:
                    self.ax_send(d, delta, 0)
        if w == 1:
            for d in both:
                self.bx_wait(d, 0)
                self.bx_send(d, 1)
            for xi in COLUMNS[1]:
                for d in both:
                    self.bz_send(d, xi, 0)
        if w == 2:
            for d in both:
                self.bx_wait(d, 1)
            for d in both:
                self.bz_send(d, 2, 0)
        if w <= 5:
            for delta in GROUPS[w - 1]:
                for d in both:
                    self.ax_wait(d, delta, 0)
                    self.ax_send(d, delta, 1)
        for u in range(3):
            t = w - 1 - u
            if 0 <= t <= 3:
                for xi in COLUMNS[u]:
                    for d in both:
                        self.bz_wait(d, xi, t)
                        if t <= 2:
                            self.bz_send(d, xi, t + 1)
        if w >= 2:
            for delta in GROUPS[w - 2]:
                for d in both:
                    self.ax_wait(d, delta, 1)

    def finish(self):
        for args in self.started:
            self.copy(*args).wait_send()


def fit_kernel(t_hbm, b_hbm, w_ref, vir_ref, bg_hbm, f_ref, bv_ref,
               t_v, tf0, tf1, tf2, cd, u, s, bg, accd, accs, fpart, fown, frecv, bvt,
               g_send, g_recv, t_send, t_recv, f_send, f_recv, one):
    z, x, y, v = position()
    o = (z * NX + x) * NY + y
    load_t = pltpu.make_async_copy(t_hbm, t_v, one.at[0])
    load_t.start()
    own = pl.ds(pl.multiple_of(o * 16, 16), 16)
    load_b = pltpu.make_async_copy(b_hbm, bg.at[own, :], one.at[1])
    load_b.start()
    barrier(peers_of(z, x, y, v))
    load_b.wait()
    swap = pltpu.make_async_remote_copy(
        src_ref=bg.at[own, :], dst_ref=bg.at[own, :], send_sem=one.at[2], recv_sem=one.at[3],
        device_id=device(z, x, 1 - y, v), device_id_type=MESH)
    swap.start()
    load_t.wait()

    labels = w_ref[...]

    def mask_row(c, _):
        row = t_v[c].astype(F32)
        row = jnp.where(labels == vir_ref[c], row, 0.0)
        for n, tf in enumerate((tf0, tf1, tf2)):
            tf[pl.ds(pl.multiple_of(c * 64, 64), 64), :] = row[:, 128 * n:128 * n + 128]
        return 0

    lax.fori_loop(0, 96, mask_row, 0)

    theirs = pl.ds(pl.multiple_of((o - y + 1 - y) * 16, 16), 16)
    pltpu.make_async_remote_copy(
        src_ref=bg.at[theirs, :], dst_ref=bg.at[theirs, :], send_sem=one.at[2], recv_sem=one.at[3],
        device_id=device(z, x, 1 - y, v), device_id_type=MESH).wait_recv()
    gather = Gather(bg, 16, 3712, g_send, g_recv)
    gather.wave(0)

    def turn(g, _):
        k = g * 4
        for n, tf in enumerate((tf0, tf1, tf2)):
            cols = pl.ds(128 * n, 128)
            rows = [tf[pl.ds(k + m, 96, stride=64), :] for m in range(4)]
            for m in range(4):
                cd[pl.ds(pl.multiple_of((k + m) * 96, 96), 96), cols] = rows[m].astype(BF16)
            for m in range(3):
                packed = jnp.concatenate([rows[m], rows[3][32 * m:32 * m + 32]], axis=0)
                u[g, m, cols, :] = packed.T.astype(BF16)
        return 0

    def t_copy(d, sb):
        to = (v + d) % NV
        return pltpu.make_async_remote_copy(
            src_ref=u.at[pl.ds(4 * sb, 4), :, pl.ds(pl.multiple_of(to * 96, 96), 96), :],
            dst_ref=s.at[pl.ds(4 * sb, 4), pl.ds(0, 3), :, pl.ds(pl.multiple_of(v * 128, 128), 128)],
            send_sem=t_send.at[d - 1, sb], recv_sem=t_recv.at[d - 1, sb],
            device_id=device(z, x, y, to), device_id_type=MESH)

    def t_wait(d, sb):
        frm = (v + NV - d) % NV
        pltpu.make_async_remote_copy(
            src_ref=u.at[pl.ds(4 * sb, 4), :, pl.ds(0, 96), :],
            dst_ref=s.at[pl.ds(4 * sb, 4), pl.ds(0, 3), :, pl.ds(pl.multiple_of(frm * 128, 128), 128)],
            send_sem=t_send.at[d - 1, sb], recv_sem=t_recv.at[d - 1, sb],
            device_id=device(z, x, y, frm), device_id_type=MESH).wait_recv()

    for sb in range(4):
        lax.fori_loop(4 * sb, 4 * sb + 4, turn, 0)
        for d in range(1, NV):
            t_copy(d, sb).start()
    mine = pltpu.make_async_copy(
        u.at[:, :, pl.ds(pl.multiple_of(v * 96, 96), 96), :],
        s.at[:, pl.ds(0, 3), :, pl.ds(pl.multiple_of(v * 128, 128), 128)], one.at[0])
    mine.start()

    pairs = ((0, 1), (7, 2), (6, 3), (5, 4))

    def zrow(delta):
        return pl.multiple_of(((z + delta) % NZ) * 128, 128)

    def times(pair, weights, acc):
        starts = [zrow(delta) for delta in pair]

        def step(kb, _):
            lanes = pl.ds(pl.multiple_of(kb * 768, 768), 768)
            left = jnp.concatenate([bg[pl.ds(a, 128), lanes] for a in starts], axis=0)
            part = jnp.dot(left, weights(kb), preferred_element_type=F32)
            for n, a in enumerate(starts):
                old = acc[pl.ds(a, 128), :]
                acc[pl.ds(a, 128), :] = jnp.where(kb == 0, 0.0, old) + part[128 * n:128 * n + 128]
            return 0

        lax.fori_loop(0, 8, step, 0)

    def out_copy(delta):
        rows = pl.ds(zrow(delta), 128)
        return pltpu.make_async_copy(bg.at[rows, :], bg_hbm.at[rows, :], one.at[4 + delta])

    def direct(n):
        times(pairs[n], lambda kb: cd[pl.ds(pl.multiple_of(kb * 768, 768), 768), :], accd)
        for delta in pairs[n]:
            out_copy(delta).start()

    def f_copy(d, delta, wait):
        lanes = pl.ds(zrow(delta), 128)
        other = (v + NV - d) % NV if wait else (v + d) % NV
        here = other if wait else v
        return pltpu.make_async_remote_copy(
            src_ref=fpart.at[other, :, lanes], dst_ref=frecv.at[here, :, lanes],
            send_sem=f_send.at[d - 1, delta], recv_sem=f_recv.at[d - 1, delta],
            device_id=device(z, x, y, other), device_id_type=MESH)

    def swapped(n):
        times(pairs[n], lambda kb: s[pl.ds(kb * 2, 2)].reshape(768, 512), accs)
        for delta in pairs[n]:
            rows = pl.ds(zrow(delta), 128)
            dt = accd[rows, :].T
            st = accs[rows, :].T
            for blk in range(NV):
                part = 2.0 * dt[96 * blk:96 * blk + 96] - st[128 * blk:128 * blk + 96]
                fpart[blk, :, rows] = part.astype(BF16)
                fown[blk, :, rows] = part
            for d in range(1, NV):
                f_copy(d, delta, False).start()

    gather.wave(1)
    gather.wave(2)
    gather.wave(3)
    direct(0)
    gather.wave(4)
    direct(1)
    gather.wave(5)
    direct(2)
    mine.wait()
    for sb in range(4):
        for d in range(1, NV):
            t_wait(d, sb)

    lane = lax.broadcasted_iota(jnp.int32, (96, 128), 1)

    def unpack(g, _):
        for blk in range(NV):
            lanes = pl.ds(128 * blk, 128)
            first = pltpu.roll(s[g, 0, :, lanes].astype(F32), 32, 1)
            second = pltpu.roll(s[g, 1, :, lanes].astype(F32), 64, 1)
            third = pltpu.roll(s[g, 2, :, lanes].astype(F32), 96, 1)
            s[g, 3, :, lanes] = jnp.where(lane < 32, first, jnp.where(lane < 64, second, third)).astype(BF16)
        return 0

    lax.fori_loop(0, 16, unpack, 0)
    for n in range(3):
        swapped(n)
    gather.wave(6)
    direct(3)
    swapped(3)

    four = bg[:, pl.ds(pl.multiple_of((o // 4) * 384, 384), 384)]
    bvt[...] = four.astype(F32).T.astype(BF16)
    bv_ref[...] = bvt[pl.ds(pl.multiple_of((o % 4) * 96, 96), 96), :]

    for d in range(1, NV):
        for delta in range(NZ):
            f_copy(d, delta, True).wait_recv()
    total = fown[v]
    for d in range(1, NV):
        total = total + frecv[(v + NV - d) % NV].astype(F32)
    f_ref[...] = total.astype(BF16)

    for d in range(1, NV):
        for delta in range(NZ):
            f_copy(d, delta, False).wait_send()
        for sb in range(4):
            t_copy(d, sb).wait_send()
    swap.wait_send()
    for delta in range(NZ):
        out_copy(delta).wait()
    gather.finish()


def cycle_kernel(bg_hbm, f_hbm, bv_hbm, r_ref,
                 bg, fg, wf, bvf, wft, bvt, g_send, g_recv, w_send, w_recv, one):
    z, x, y, v = position()
    o = (z * NX + x) * NY + y
    load = pltpu.make_async_copy(bg_hbm, bg, one.at[0])
    load.start()
    own = pl.ds(pl.multiple_of(o * 96, 96), 96)
    mine = pl.ds(pl.multiple_of(v * 96, 96), 96)
    loads = [
        pltpu.make_async_copy(f_hbm, fg.at[own, :], one.at[1]),
        pltpu.make_async_copy(f_hbm, wf.at[mine, :], one.at[2]),
        pltpu.make_async_copy(bv_hbm, bvf.at[mine, :], one.at[3]),
    ]
    for copy in loads:
        copy.start()
    barrier(peers_of(z, x, y, v))
    for copy in loads:
        copy.wait()

    def swap_copy(there):
        rows = pl.ds(pl.multiple_of((o - y + there) * 96, 96), 96)
        return pltpu.make_async_remote_copy(
            src_ref=fg.at[rows, :], dst_ref=fg.at[rows, :], send_sem=one.at[4], recv_sem=one.at[5],
            device_id=device(z, x, 1 - y, v), device_id_type=MESH)

    swap_copy(y).start()

    def w_copy(d, which, wait):
        ref = (wf, bvf)[which]
        other = (v + NV - d) % NV if wait else (v + d) % NV
        rows = pl.ds(pl.multiple_of((other if wait else v) * 96, 96), 96)
        return pltpu.make_async_remote_copy(
            src_ref=ref.at[rows, :], dst_ref=ref.at[rows, :], send_sem=w_send.at[which, d - 1],
            recv_sem=w_recv.at[which, d - 1], device_id=device(z, x, y, other), device_id_type=MESH)

    for which in range(2):
        for d in range(1, NV):
            w_copy(d, which, False).start()
    swap_copy(1 - y).wait_recv()
    gather = Gather(fg, 96, 640, g_send, g_recv)
    gather.wave(0)
    for d in range(1, NV):
        w_copy(d, 0, True).wait_recv()
    wft[...] = wf[...].astype(F32).T.astype(BF16)
    load.wait()

    def direct(n, _):
        lanes = pl.ds(pl.multiple_of(n * 384, 384), 384)
        part = lax.dot_general(bg[:, lanes], wft[...], (((0,), (0,)), ((), ())), preferred_element_type=F32)
        r_ref[pl.ds(pl.multiple_of(n * 384, 384), 384), :] = part.astype(BF16)
        return 0

    def mirror(delta):
        start = pl.multiple_of(((z + delta) % NZ) * 768, 768)

        def step(n, _):
            rows = pl.ds(pl.multiple_of(start + n * 384, 384), 384)
            part = jnp.dot(fg[rows, :], bvt[...], preferred_element_type=F32)
            r_ref[rows, :] = (r_ref[rows, :].astype(F32) + part).astype(BF16)
            return 0

        lax.fori_loop(0, 2, step, 0)

    lax.fori_loop(0, 4, direct, 0)
    gather.wave(1)
    lax.fori_loop(4, 8, direct, 0)
    gather.wave(2)
    lax.fori_loop(8, 12, direct, 0)
    gather.wave(3)
    lax.fori_loop(12, 16, direct, 0)
    for d in range(1, NV):
        w_copy(d, 1, True).wait_recv()
    bvt[...] = bvf[...].astype(F32).T.astype(BF16)
    gather.wave(4)
    for t in range(3):
        for delta in GROUPS[t]:
            mirror(delta)
    gather.wave(5)
    for delta in GROUPS[3]:
        mirror(delta)
    gather.wave(6)
    mirror(4)

    swap_copy(y).wait_send()
    for which in range(2):
        for d in range(1, NV):
            w_copy(d, which, False).wait_send()
    gather.finish()


def on_device(amplitudes, aux_ints, occ_irrep, vir_irrep):
    o, v = lax.axis_index("occ"), lax.axis_index("vir")
    labels = lax.dynamic_slice_in_dim(occ_irrep, o, 1)[:, None] ^ occ_irrep[:, None] ^ vir_irrep[None, :]
    block = lax.dynamic_slice_in_dim(vir_irrep, v * 96, 96)
    shard = jnp.transpose(aux_ints, (2, 1, 0)).reshape(16, 6144)
    any_spec = pl.BlockSpec(memory_space=pl.ANY)
    vmem_spec = pl.BlockSpec(memory_space=pltpu.VMEM)
    dma, vmem = pltpu.SemaphoreType.DMA, pltpu.VMEM
    bg, f, bv = pl.pallas_call(
        fit_kernel,
        name="fit",
        out_shape=(
            jax.ShapeDtypeStruct((1024, 6144), BF16),
            jax.ShapeDtypeStruct((96, 1024), BF16),
            jax.ShapeDtypeStruct((96, 1024), BF16),
        ),
        in_specs=[any_spec, any_spec, vmem_spec, pl.BlockSpec(memory_space=pltpu.SMEM)],
        out_specs=(any_spec, vmem_spec, vmem_spec),
        scratch_shapes=[
            vmem((96, 64, 384), BF16), vmem((6144, 128), F32), vmem((6144, 128), F32), vmem((6144, 128), F32),
            vmem((6144, 384), BF16),
            vmem((16, 3, 384, 128), BF16), vmem((16, 4, 96, 512), BF16), vmem((1024, 6144), BF16),
            vmem((1024, 384), F32), vmem((1024, 512), F32), vmem((NV, 96, 1024), BF16),
            vmem((NV, 96, 1024), F32), vmem((NV, 96, 1024), BF16), vmem((384, 1024), BF16),
            dma((N_SEMS,)), dma((N_SEMS,)), dma((3, 4)), dma((3, 4)), dma((3, 8)), dma((3, 8)), dma((12,)),
        ],
        compiler_params=pltpu.CompilerParams(collective_id=0, has_side_effects=True, vmem_limit_bytes=60 << 20),
    )(amplitudes[0], shard, labels, block)
    r = pl.pallas_call(
        cycle_kernel,
        name="cycle",
        out_shape=jax.ShapeDtypeStruct((6144, 384), BF16),
        in_specs=[any_spec, any_spec, any_spec],
        out_specs=vmem_spec,
        scratch_shapes=[
            vmem((1024, 6144), BF16), vmem((6144, 1024), BF16), vmem((384, 1024), BF16), vmem((384, 1024), BF16),
            vmem((1024, 384), BF16), vmem((1024, 384), BF16),
            dma((N_SEMS,)), dma((N_SEMS,)), dma((2, 3)), dma((2, 3)), dma((6,)),
        ],
        compiler_params=pltpu.CompilerParams(collective_id=1, has_side_effects=True, vmem_limit_bytes=60 << 20),
    )(bg, f, bv)
    return jnp.transpose(r.reshape(64, 96, 384), (1, 0, 2))[None]


def solution(mesh):
    in_specs = (P("occ", "vir", None, None), P("vir", None, "occ"), P(), P())
    out_specs = P("occ", "vir", None, None)
    return jax.shard_map(
        on_device, mesh=mesh, in_specs=in_specs, out_specs=out_specs, check_vma=False
    )
```

time: 549 us -> 214 us (0.39)
  blocking collectives: 317 us -> 0 us
  Pallas kernels: 0 us -> 200 us
  waiting for transfers between devices: 98.6 us -> 0 us
  local copies, waits for them, and re-layouts: 66 us -> 10.8 us
  matrix products: 29.1 us -> 0 us
  other arithmetic: 23.4 us -> 2.71 us
  between operations: 13.4 us -> 0.02 us
    all_to_all x3 -> x0, blocking collectives: 282 us -> none  [the longest x1 114 us: on_device(): lax.all_to_all(cycle_term, 'occ', split_axis=2, concat_axis=0, tiled=True)]
    pallas_call x0 -> x2, Pallas kernels: none -> 200 us  [the longest x1 111 us: on_device(): pl.pallas_call(fit_kernel, name='fit', out_shape=(jax.ShapeDtypeStruct((1...]
    all_gather x1 -> x0, waiting for transfers between devices: 97.9 us -> none  [on_device(): gathered = lax.all_gather(aux_ints, 'occ', axis=2, tiled=True)]
    convert_element_type x4 -> x0, local copies, waits for them, and re-layouts: 45.1 us -> none  [the longest x2 26 us: on_device(): mirror.astype(jnp.float32)]
    psum x1 -> x0, blocking collectives: 34.8 us -> none  [on_device(): summed = lax.psum(partial_value, 'vir')]
    dot_general x2 -> x0, matrix products: 29.1 us -> none  [the longest x1 18.3 us: on_device(): jnp.einsum('icka,ckp->iap', combined, gathered, preferred_element_type=jn...]
    unnamed x7 -> x0, local copies, waits for them, and re-layouts: 11.7 us -> none
    another operation x1 -> x0, other arithmetic: 11.3 us -> none
  transfers between devices with their start and end apart: 1 -> 0, of which waited for: 1 -> 0; matrix products, arithmetic and copies ran while one was open for 8% -> 0% of each run, Pallas kernels for 0% -> 0%
where the time goes in v1:
time: 214 us; the launch traced here: 213 us
  Pallas kernels  200 us (93%)
  local copies, waits for them, and re-layouts  10.8 us (5%)
  other arithmetic  2.71 us (1%)
    pallas_call x1, Pallas kernels, on_device(): pl.pallas_call(fit_kernel, name='fit', out_shape=(jax.ShapeDtypeStruct((1...  111 us
    pallas_call x1, Pallas kernels, on_device(): pl.pallas_call(cycle_kernel, name='cycle', out_shape=jax.ShapeDtypeStruct...  89 us
    reshape x1, local copies, waits for them, and re-layouts, on_device(): return jnp.transpose(r.reshape(64, 96, 384), (1, 0, 2))[None]  6.24 us

profile of v1, /device:TPU:1, one launch (start us, length us, event | category | flops | bytes accessed | tf_op | source)
XLA Modules:
  0.0 213.5 jit_solution(14148986561640078028)
XLA Ops:
  0.0 1.2 dynamic_slice.6
  1.2 1.3 broadcast_xor_fusion.1
  2.5 1.3 dynamic_slice.7.vir_ref
  3.9 1.4 broadcast_xor_fusion.w_ref
  5.3 1.0 copy.5
  6.3 1.0 reshape.12.b_hbm
  7.3 110.9 %fit.1 = (bf16[1024,6144]{1,0:T(8,128)(2,1)}, bf16[96,1024]{1,0:T(8,128)(2,1)}, bf16[96,1024]{1,0:T(8,128)(2,1)}) custom-call(bf16[96,64,384]{2,1,0:T(8,128)(2,1)} %bitcast.10, bf16[16,6144]{1,0:T(8,128)(2,1)} %reshape.12.b_hbm, s32[64,384]{1,0:T(8,128)} %broadcast_xor_fusion.w_ref, s32[96]{0:T(128)} %dynamic_slice.7.vir_ref), custom_call_target="tpu_custom_call" | custom-call | tf_op jit(solution)/shard_map/fit/pallas_call | solution.py:463
  118.2 89.0 %cycle.1 = bf16[6144,384]{1,0:T(8,128)(2,1)} custom-call(bf16[1024,6144]{1,0:T(8,128)(2,1)} %get-tuple-element.8.bg_hbm, bf16[96,1024]{1,0:T(8,128)(2,1)} %get-tuple-element.9.f_hbm, bf16[96,1024]{1,0:T(8,128)(2,1)} %get-tuple-element.10.bv_hbm), custom_call_target="tpu_custom_call" | custom-call | tf_op jit(solution)/shard_map/cycle/pallas_call | solution.py:483
  207.2 6.2 %copy.8 = bf16[64,96,384]{2,0,1:T(8,128)(2,1)} copy(bf16[64,96,384]{2,1,0:T(8,128)(2,1)} %bitcast.9) | data formatting | bytes 9437184 | tf_op jit(solution)/shard_map/reshape | solution.py:496

commit v2 on v0

v2 whole, which is shorter than its diff:
```python
import functools

import jax
import jax.numpy as jnp
from jax import lax
from jax.experimental import pallas as pl
from jax.experimental.pallas import tpu as pltpu
from jax.sharding import PartitionSpec as P

MESH = pl.DeviceIdType.MESH
NZ, NX, NY, NV = 8, 4, 2, 4
BF16, F32 = jnp.bfloat16, jnp.float32
GROUPS = ((0,), (1, 7), (2, 6), (3, 5), (4,))
COLUMNS = ((0,), (1, 3), (2,))
N_SEMS = 84


def position():
    o, v = lax.axis_index("occ"), lax.axis_index("vir")
    return o // (NX * NY), (o // NY) % NX, o % NY, v


def device(z, x, y, v):
    return ((z * NX + x) * NY + y, v)


def barrier(peers):
    sem = pltpu.get_barrier_semaphore()
    for peer in peers:
        pl.semaphore_signal(sem, 1, device_id=peer, device_id_type=MESH)
    pl.semaphore_wait(sem, len(peers))


def peers_of(z, x, y, v):
    ring = [
        device((z + 1) % NZ, x, y, v),
        device((z + NZ - 1) % NZ, x, y, v),
        device(z, (x + 1) % NX, y, v),
        device(z, (x + NX - 1) % NX, y, v),
        device(z, x, 1 - y, v),
    ]
    return ring + [device(z, x, y, (v + d) % NV) for d in range(1, NV)]


class Gather:
    def __init__(self, ref, block, region, two_pieces, send_sems, recv_sems):
        self.ref, self.block, self.region, self.two_pieces = ref, block, region, two_pieces
        self.send_sems, self.recv_sems = send_sems, recv_sems
        self.z, self.x, self.y, self.v = position()
        self.started = []

    def copy(self, key, z, x, half, piece):
        kind, d = key[0], key[1]
        if kind == "az":
            index = d * 4 + key[2]
        elif kind == "ax":
            index = 8 + (d * 8 + key[2]) * 2 + key[3]
        elif kind == "bx":
            index = 40 + d * 2 + key[2]
        else:
            index = 44 + (d * 4 + key[2]) * 4 + key[3]
        if piece == 1:
            index = 76 + {"az": 0, "ax": 1, "bx": 2, "bz": 3}[kind] * 2 + d
        (start, size), lanes = self.region(kind[0], half, piece)
        rows = pl.ds(pl.multiple_of((z % NZ * NX + x % NX) * self.block + start, 16), size)
        part = self.ref.at[rows, lanes]
        s = 1 - 2 * d
        if kind[1] == "z":
            target = device((self.z + s + NZ) % NZ, self.x, self.y, self.v)
        else:
            target = device(self.z, (self.x + s + NX) % NX, self.y, self.v)
        return pltpu.make_async_remote_copy(
            src_ref=part, dst_ref=part, send_sem=self.send_sems.at[index],
            recv_sem=self.recv_sems.at[index], device_id=target, device_id_type=MESH)

    def place(self, key, behind):
        kind, d = key[0], key[1]
        s = 1 - 2 * d
        half = None
        if kind == "az":
            dz, dx = -s * (key[2] + behind), 0
            half = d if key[2] == 3 else None
        elif kind == "ax":
            dz, dx = key[2], -s * (key[3] + behind)
            half = d if key[3] == 1 else None
        elif kind == "bx":
            dz, dx = 0, -s * (key[2] + behind)
            half = d if key[2] == 1 else None
        else:
            dz, dx = -s * (key[3] + behind), key[2]
            half = d if key[3] == 3 else None
        return self.z + dz + NZ, self.x + dx + NX, half

    def pieces(self, key):
        own = key[2:] in ((0,), (0, 0))
        if not own:
            return (None,)
        return (0, 1) if key[0][0] in self.two_pieces else (0,)

    def send(self, *key, piece=None):
        z, x, half = self.place(key, 0)
        self.copy(key, z, x, half, piece).start()
        self.started.append((key, piece))

    def wait(self, *key):
        z, x, half = self.place(key, 1)
        for piece in self.pieces(key):
            self.copy(key, z, x, half, piece).wait_recv()

    def own(self, piece):
        for kind in (("az", "bx"), ("ax", "bz")):
            for d in (0, 1):
                for name in kind:
                    key = (name, d, 0) if name in ("az", "bx") else (name, d, 0, 0)
                    if piece in self.pieces(key):
                        self.send(*key, piece=piece)

    def wave(self, w):
        both = (0, 1)
        if w <= 4:
            for d in both:
                self.wait("az", d, w - 1)
                if w <= 3:
                    self.send("az", d, w)
            for delta in GROUPS[w]:
                for d in both:
                    self.send("ax", d, delta, 0)
        if w == 1:
            for d in both:
                self.wait("bx", d, 0)
                self.send("bx", d, 1)
            for xi in COLUMNS[1]:
                for d in both:
                    self.send("bz", d, xi, 0)
        if w == 2:
            for d in both:
                self.wait("bx", d, 1)
            for d in both:
                self.send("bz", d, 2, 0)
        for delta in GROUPS[w - 1]:
            for d in both:
                self.wait("ax", d, delta, 0)
                self.send("ax", d, delta, 1)
        for u in range(3):
            t = w - 1 - u
            if 0 <= t <= 2:
                for xi in COLUMNS[u]:
                    for d in both:
                        self.wait("bz", d, xi, t)
                        self.send("bz", d, xi, t + 1)

    def settle(self, t, kinds="ab"):
        if "b" in kinds and t == 4:
            for xi in range(4):
                for d in (0, 1):
                    self.wait("bz", d, xi, 3)
        if "a" in kinds:
            for delta in GROUPS[t]:
                for d in (0, 1):
                    self.wait("ax", d, delta, 1)

    def finish(self):
        for key, piece in self.started:
            z, x, half = self.place(key, 0)
            self.copy(key, z, x, half, piece).wait_send()


def kernel(t_hbm, b_ref, occ_ref, vir_ref, vrow_ref, r_hbm,
           r_v, tf0, tf1, tf2, cd, u, s, bg, acc, fpart, fown, frecv, bvt, labels,
           fg, wf, bvf, rsend, rrecv,
           g_send, g_recv, g2_send, g2_recv, t_send, t_recv, f_send, f_recv,
           w_send, w_recv, v_send, v_recv, r_sem, rr_sem, one):
    z, x, y, v = position()
    o = (z * NX + x) * NY + y
    load_t = pltpu.make_async_copy(t_hbm, r_v, one.at[0])
    load_t.start()
    own = pl.ds(pl.multiple_of(o * 16, 16), 16)

    def place_b(n, _):
        four = jnp.concatenate([b_ref[4 * n + m].astype(F32) for m in range(4)], axis=1)
        bg[own, pl.ds(pl.multiple_of(n * 384, 384), 384)] = four.astype(BF16)
        return 0

    lax.fori_loop(0, 16, place_b, 0)
    barrier(peers_of(z, x, y, v))

    def swap_copy(there):
        rows = pl.ds(pl.multiple_of((o - y + there) * 16, 16), 16)
        return pltpu.make_async_remote_copy(
            src_ref=bg.at[rows, :], dst_ref=bg.at[rows, :], send_sem=one.at[2], recv_sem=one.at[3],
            device_id=device(z, x, 1 - y, v), device_id_type=MESH)

    def region(kind, half, piece):
        if piece is not None:
            rows = ((y if piece == 0 else 1 - y) * 16, 16)
        elif half is not None:
            rows = (half * 16, 16)
        else:
            rows = (0, 32)
        return rows, pl.ds(0, 3712) if kind == "a" else pl.ds(3712, 6144 - 3712)

    swap_copy(y).start()
    gather = Gather(bg, 32, region, "ab", g_send, g_recv)
    gather.own(0)

    mine_label = occ_ref[o]
    vrow = vrow_ref[...]

    def label_row(k, _):
        labels[pl.ds(k, 1), :] = vrow ^ (occ_ref[k] ^ mine_label)
        return 0

    lax.fori_loop(0, 64, label_row, 0)
    load_t.wait()

    def mask_row(c, _):
        row = r_v[pl.ds(pl.multiple_of(c * 64, 64), 64), :].astype(F32)
        row = jnp.where(labels[...] == vir_ref[v * 96 + c], row, 0.0)
        for n, tf in enumerate((tf0, tf1, tf2)):
            tf[pl.ds(pl.multiple_of(c * 64, 64), 64), :] = row[:, 128 * n:128 * n + 128]
        return 0

    lax.fori_loop(0, 96, mask_row, 0)
    swap_copy(1 - y).wait_recv()
    gather.own(1)

    lane = lax.broadcasted_iota(jnp.int32, (96, 128), 1)

    def turn(g, _):
        k = g * 4
        rows = [[tf[pl.ds(k + m, 96, stride=64), :] for tf in (tf0, tf1, tf2)] for m in range(4)]
        for n in range(3):
            for m in range(3):
                packed = jnp.concatenate([rows[m][n], rows[3][n][32 * m:32 * m + 32]], axis=0)
                u[g, m, pl.ds(128 * n, 128), :] = packed.T.astype(BF16)
        for m in range(4):
            a, b, c = rows[m]
            into = pl.ds(pl.multiple_of((k + m) * 96, 96), 96)
            cd[into, pl.ds(0, 128)] = a.astype(BF16)
            cd[into, pl.ds(128, 128)] = jnp.where(
                lane < 32, pltpu.roll(a, 32, 1), pltpu.roll(b, 32, 1)).astype(BF16)
            cd[into, pl.ds(256, 128)] = jnp.where(
                lane < 64, pltpu.roll(b, 64, 1), pltpu.roll(c, 64, 1)).astype(BF16)
            cd[into, pl.ds(384, 128)] = pltpu.roll(c, 96, 1).astype(BF16)
        return 0

    def t_copy(d, sb, wait=False):
        other = (v + NV - d) % NV if wait else (v + d) % NV
        here = other if wait else v
        return pltpu.make_async_remote_copy(
            src_ref=u.at[pl.ds(4 * sb, 4), :, pl.ds(pl.multiple_of(other * 96, 96), 96), :],
            dst_ref=s.at[pl.ds(4 * sb, 4), pl.ds(0, 3), :, pl.ds(pl.multiple_of(here * 128, 128), 128)],
            send_sem=t_send.at[d - 1, sb], recv_sem=t_recv.at[d - 1, sb],
            device_id=device(z, x, y, other), device_id_type=MESH)

    for sb in range(4):
        lax.fori_loop(4 * sb, 4 * sb + 4, turn, 0)
        for d in range(1, NV):
            t_copy(d, sb).start()
    mine = pltpu.make_async_copy(
        u.at[:, :, pl.ds(pl.multiple_of(v * 96, 96), 96), :],
        s.at[:, pl.ds(0, 3), :, pl.ds(pl.multiple_of(v * 128, 128), 128)], one.at[0])
    mine.start()

    pairs = ((0, 1), (7, 2), (6, 3), (5, 4))

    def zrow(delta):
        return pl.multiple_of(((z + delta) % NZ) * 128, 128)

    def combine(g, _):
        for blk in range(NV):
            lanes = pl.ds(128 * blk, 128)
            got = [s[g, m, :, lanes].astype(F32) for m in range(3)]
            last = jnp.where(lane < 32, pltpu.roll(got[0], 32, 1), jnp.where(
                lane < 64, pltpu.roll(got[1], 64, 1), pltpu.roll(got[2], 96, 1)))
            for m, other in enumerate(got + [last]):
                straight = cd[pl.ds(pl.multiple_of((4 * g + m) * 96, 96), 96), lanes].astype(F32)
                s[g, m, :, lanes] = (2.0 * straight - other).astype(BF16)
        return 0

    def pick(n):
        for delta in pairs[n]:
            rows = pl.ds(zrow(delta), 128)
            four = bg[rows, pl.ds(pl.multiple_of((o // 4) * 384, 384), 384)]
            bvt[:, rows] = four.astype(F32).T.astype(BF16)

    def f_copy(d, delta, wait):
        lanes = pl.ds(zrow(delta), 128)
        other = (v + NV - d) % NV if wait else (v + d) % NV
        here = other if wait else v
        return pltpu.make_async_remote_copy(
            src_ref=fpart.at[other, :, lanes], dst_ref=frecv.at[here, :, lanes],
            send_sem=f_send.at[d - 1, delta], recv_sem=f_recv.at[d - 1, delta],
            device_id=device(z, x, y, other), device_id_type=MESH)

    def fit(n):
        starts = [zrow(delta) for delta in pairs[n]]

        def step(kb, _):
            lanes = pl.ds(pl.multiple_of(kb * 768, 768), 768)
            left = jnp.concatenate([bg[pl.ds(a, 128), lanes] for a in starts], axis=0)
            part = jnp.dot(left, s[pl.ds(kb * 2, 2)].reshape(768, 512), preferred_element_type=F32)
            acc[...] = jnp.where(kb == 0, 0.0, acc[...]) + part
            return 0

        lax.fori_loop(0, 8, step, 0)
        for m, delta in enumerate(pairs[n]):
            rows = pl.ds(zrow(delta), 128)
            turned = acc[pl.ds(128 * m, 128), :].T
            for blk in range(NV):
                part = turned[128 * blk:128 * blk + 96]
                fpart[blk, :, rows] = part.astype(BF16)
                fown[blk, :, rows] = part
            for d in range(1, NV):
                f_copy(d, delta, False).start()

    gather.wave(1)
    gather.wave(2)
    gather.wave(3)
    gather.settle(0)
    gather.settle(1)
    pick(0)
    gather.wave(4)
    gather.settle(2)
    pick(1)
    mine.wait()
    for sb in range(4):
        for d in range(1, NV):
            t_copy(d, sb, True).wait_recv()
    lax.fori_loop(0, 16, combine, 0)
    fit(0)
    gather.wave(5)
    fit(1)
    gather.settle(3)
    fit(2)
    gather.settle(4)
    fit(3)
    pick(2)
    pick(3)
    two = pl.ds(pl.multiple_of((o % 4 - y) * 96, 96), 192)
    same = pltpu.make_async_copy(bvt.at[two, :], bvf.at[pl.ds(pl.multiple_of(v * 192, 192), 192), :], one.at[0])
    same.start()

    for d in range(1, NV):
        for delta in range(NZ):
            f_copy(d, delta, True).wait_recv()
    total = fown[v]
    for d in range(1, NV):
        total = total + frecv[(v + NV - d) % NV].astype(F32)
    total = total.astype(BF16)
    block = pl.multiple_of((z * NX + x) * 128, 128)
    fg[pl.ds(block, 96), :] = total
    wf[pl.ds(pl.multiple_of(v * 96, 96), 96), :] = total

    swap = pltpu.make_async_remote_copy(
        src_ref=fg.at[pl.ds(block + 64, 32), :], dst_ref=fg.at[pl.ds(block + 96, 32), :],
        send_sem=one.at[4], recv_sem=one.at[5], device_id=device(z, x, 1 - y, v), device_id_type=MESH)
    swap.start()

    mate, across = v + 1 - 2 * (v % 2), (v + 2) % NV
    far = (mate + 2) % NV

    def share(ref, size, send_sems, recv_sems, step, blk):
        rows = pl.ds(pl.multiple_of(blk * size, size), size)
        return pltpu.make_async_remote_copy(
            src_ref=ref.at[rows, :], dst_ref=ref.at[rows, :], send_sem=send_sems.at[step], recv_sem=recv_sems.at[step],
            device_id=device(z, x, y, across if step == 1 else mate), device_id_type=MESH)

    def region2(kind, half, piece):
        if kind == "b":
            rows = (0, 64) if half is None else (32 * half, 32)
        elif piece is not None:
            rows = (64 + 32 * piece, 32)
        else:
            rows = (64, 64) if half is None else (64 + 32 * half, 32)
        return rows, pl.ds(0, 1024)

    again = Gather(fg, 128, region2, "a", g2_send, g2_recv)
    again.own(0)
    same.wait()
    shares = ((bvf, 192, v_send, v_recv), (wf, 96, w_send, w_recv))
    for share_args in shares:
        share(*share_args, 1, v).start()
        share(*share_args, 0, v).start()
    swap.wait_recv()
    again.own(1)
    for share_args in shares:
        share(*share_args, 1, across).wait_recv()
        share(*share_args, 2, across).start()
        if share_args is shares[0]:
            again.wave(1)
    share(*shares[0], 0, mate).wait_recv()
    share(*shares[0], 2, far).wait_recv()
    first, second, third = (cd.at[pl.ds(1024 * n, 1024), pl.ds(0, 384)] for n in range(3))
    for ref, which in ((second, 1 - y), (first, y)):
        whole = jnp.concatenate(
            [bvf[pl.ds(pl.multiple_of(blk * 192 + which * 96, 96), 96), :] for blk in range(NV)], axis=0)
        ref[...] = whole.astype(F32).T.astype(BF16)

    def direct(n, _):
        lanes = pl.ds(pl.multiple_of(n * 384, 384), 384)
        part = lax.dot_general(bg[:, lanes], third[...], (((0,), (0,)), ((), ())), preferred_element_type=F32)
        r_v[pl.ds(pl.multiple_of(n * 384, 384), 384), :] = part.astype(BF16)
        return 0

    def add(row, size, part):
        rows = pl.ds(pl.multiple_of(row, 32), size)
        r_v[rows, :] = (r_v[rows, :].astype(F32) + part).astype(BF16)

    def r_copy(delta):
        rows = pl.ds(pl.multiple_of(((z + delta) % NZ) * 256, 256), 256)
        return pltpu.make_async_remote_copy(
            src_ref=rsend.at[rows, :], dst_ref=rrecv.at[rows, :], send_sem=r_sem.at[delta],
            recv_sem=rr_sem.at[delta], device_id=device(z, x, 1 - y, v), device_id_type=MESH)

    def theirs(t):
        for delta in GROUPS[t]:
            zz = (z + delta) % NZ
            left = jnp.concatenate(
                [fg[pl.ds(pl.multiple_of(zz * 512 + 128 * m, 128), 64), :] for m in range(NX)], axis=0)
            part = jnp.dot(left, second[...], preferred_element_type=F32)
            rsend[pl.ds(pl.multiple_of(zz * 256, 256), 256), :] = part.astype(BF16)
            r_copy(delta).start()

    def ours(t):
        for delta in GROUPS[t]:
            zz = (z + delta) % NZ
            rows = pl.ds(pl.multiple_of(zz * 512, 512), 512)
            part = jnp.dot(fg[rows, :], first[...], preferred_element_type=F32)
            for m in range(NX):
                pair = (zz * NX + m) * NY
                add((pair + y) * 96, 96, part[128 * m:128 * m + 96])
                add((pair + 1 - y) * 96 + 64, 32, part[128 * m + 96:128 * m + 128])

    def arrived(t):
        for delta in GROUPS[t]:
            r_copy(delta).wait_recv()
            zz = (z + delta) % NZ
            for m in range(NX):
                got = rrecv[pl.ds(pl.multiple_of(zz * 256 + 64 * m, 64), 64), :].astype(F32)
                add(((zz * NX + m) * NY + 1 - y) * 96, 64, got)

    again.wave(2)
    theirs(0)
    share(*shares[1], 0, mate).wait_recv()
    share(*shares[1], 2, far).wait_recv()
    third[...] = wf[...].astype(F32).T.astype(BF16)
    lax.fori_loop(0, 4, direct, 0)
    again.wave(3)
    theirs(1)
    lax.fori_loop(4, 10, direct, 0)
    again.wave(4)
    theirs(2)
    lax.fori_loop(10, 16, direct, 0)
    again.settle(0, "a")
    ours(0)
    again.settle(1, "a")
    ours(1)
    again.wave(5)
    theirs(3)
    again.settle(4, "b")
    theirs(4)
    for t in range(2, 5):
        again.settle(t, "a")
        ours(t)
        arrived(t - 2)
    arrived(3)
    arrived(4)
    save = pltpu.make_async_copy(r_v, r_hbm, one.at[0])
    save.start()

    for d in range(1, NV):
        for delta in range(NZ):
            f_copy(d, delta, False).wait_send()
        for sb in range(4):
            t_copy(d, sb).wait_send()
    swap_copy(y).wait_send()
    gather.finish()
    swap.wait_send()
    for share_args in shares:
        for step in range(3):
            share(*share_args, step, across if step == 2 else v).wait_send()
    for delta in range(NZ):
        r_copy(delta).wait_send()
    again.finish()
    save.wait()


def on_device(amplitudes, aux_ints, occ_irrep, vir_irrep):
    any_spec = pl.BlockSpec(memory_space=pl.ANY)
    vmem_spec = pl.BlockSpec(memory_space=pltpu.VMEM)
    smem_spec = pl.BlockSpec(memory_space=pltpu.SMEM)
    dma, vmem = pltpu.SemaphoreType.DMA, pltpu.VMEM
    r = pl.pallas_call(
        kernel,
        name="ccsd",
        out_shape=jax.ShapeDtypeStruct((6144, 384), BF16),
        in_specs=[any_spec, vmem_spec, smem_spec, smem_spec, vmem_spec],
        out_specs=any_spec,
        scratch_shapes=[
            vmem((6144, 384), BF16), vmem((6144, 128), F32), vmem((6144, 128), F32), vmem((6144, 128), F32),
            vmem((6144, 512), BF16), vmem((16, 3, 384, 128), BF16), vmem((16, 4, 96, 512), BF16),
            vmem((1024, 6144), BF16), vmem((256, 512), F32), vmem((NV, 96, 1024), BF16),
            vmem((NV, 96, 1024), F32), vmem((NV, 96, 1024), BF16), vmem((384, 1024), BF16),
            vmem((64, 384), jnp.int32),
            vmem((4096, 1024), BF16), vmem((384, 1024), BF16), vmem((768, 1024), BF16),
            vmem((2048, 384), BF16), vmem((2048, 384), BF16),
            dma((N_SEMS,)), dma((N_SEMS,)), dma((N_SEMS,)), dma((N_SEMS,)),
            dma((3, 4)), dma((3, 4)), dma((3, 8)), dma((3, 8)),
            dma((3,)), dma((3,)), dma((3,)), dma((3,)), dma((8,)), dma((8,)), dma((6,)),
        ],
        compiler_params=pltpu.CompilerParams(collective_id=0, has_side_effects=True, vmem_limit_bytes=63 << 20),
    )(amplitudes.reshape(6144, 384), jnp.transpose(aux_ints, (1, 2, 0)), occ_irrep, vir_irrep, vir_irrep[None, :])
    return jnp.transpose(r.reshape(64, 96, 384), (1, 0, 2))[None]


def solution(mesh):
    in_specs = (P("occ", "vir", None, None), P("vir", None, "occ"), P(), P())
    out_specs = P("occ", "vir", None, None)
    return jax.shard_map(
        on_device, mesh=mesh, in_specs=in_specs, out_specs=out_specs, check_vma=False
    )
```

time: 549 us -> 182 us (0.33)
  blocking collectives: 317 us -> 0 us
  Pallas kernels: 0 us -> 173 us
  waiting for transfers between devices: 98.6 us -> 0 us
  local copies, waits for them, and re-layouts: 66 us -> 7.48 us
  matrix products: 29.1 us -> 0 us
  other arithmetic: 23.4 us -> 0 us
  between operations: 13.4 us -> 0.01 us
    all_to_all x3 -> x0, blocking collectives: 282 us -> none  [the longest x1 114 us: on_device(): lax.all_to_all(cycle_term, 'occ', split_axis=2, concat_axis=0, tiled=True)]
    pallas_call x0 -> x1, Pallas kernels: none -> 173 us  [on_device(): pl.pallas_call(kernel, name='ccsd', out_shape=jax.ShapeDtypeStruct((6144,...]
    all_gather x1 -> x0, waiting for transfers between devices: 97.9 us -> none  [on_device(): gathered = lax.all_gather(aux_ints, 'occ', axis=2, tiled=True)]
    convert_element_type x4 -> x0, local copies, waits for them, and re-layouts: 45.1 us -> none  [the longest x2 26 us: on_device(): mirror.astype(jnp.float32)]
    psum x1 -> x0, blocking collectives: 34.8 us -> none  [on_device(): summed = lax.psum(partial_value, 'vir')]
    dot_general x2 -> x0, matrix products: 29.1 us -> none  [the longest x1 18.3 us: on_device(): jnp.einsum('icka,ckp->iap', combined, gathered, preferred_element_type=jn...]
    unnamed x7 -> x0, local copies, waits for them, and re-layouts: 11.7 us -> none
    another operation x1 -> x0, other arithmetic: 11.3 us -> none
  transfers between devices with their start and end apart: 1 -> 0, of which waited for: 1 -> 0; matrix products, arithmetic and copies ran while one was open for 8% -> 0% of each run, Pallas kernels for 0% -> 0%
where the time goes in v2:
time: 182 us; the launch traced here: 181 us
  Pallas kernels  173 us (95%)
  local copies, waits for them, and re-layouts  7.48 us (4%)
    pallas_call x1, Pallas kernels, on_device(): pl.pallas_call(kernel, name='ccsd', out_shape=jax.ShapeDtypeStruct((6144,...  173 us
    reshape x1, local copies, waits for them, and re-layouts, on_device(): return jnp.transpose(r.reshape(64, 96, 384), (1, 0, 2))[None]  6.24 us

profile of v2, /device:TPU:1, one launch (start us, length us, event | category | flops | bytes accessed | tf_op | source)
XLA Modules:
  0.0 181.0 jit_solution(6134650606049218771)
XLA Ops:
  0.0 1.2 broadcast_in_dim.6.vrow_ref
  1.2 173.5 %ccsd.1 = bf16[6144,384]{1,0:T(8,128)(2,1)} custom-call(bf16[6144,384]{1,0:T(8,128)(2,1)} %bitcast.9, bf16[64,16,96]{2,1,0:T(8,128)(2,1)} %bitcast.10, s32[64]{0:T(128)} %occ_ref.1, s32[384]{0:T(512)} %vir_ref.1, s32[1,384]{1,0:T(1,128)} %broadcast_in_dim.6.vrow_ref), custom_call_target="tpu_custom_call" | custom-call | tf_op jit(solution)/shard_map/ccsd/pallas_call | solution.py:494
  174.7 6.2 %copy.7 = bf16[64,96,384]{2,0,1:T(8,128)(2,1)} copy(bf16[64,96,384]{2,1,0:T(8,128)(2,1)} %bitcast.8) | data formatting | bytes 9437184 | tf_op jit(solution)/shard_map/reshape | solution.py:514

commit v3 on v2

--- a/solution.py
+++ b/solution.py
@@ -149,15 +149,15 @@
                         self.wait("bz", d, xi, t)
                         self.send("bz", d, xi, t + 1)
 
-    def settle(self, t, kinds="ab"):
-        if "b" in kinds and t == 4:
-            for xi in range(4):
-                for d in (0, 1):
-                    self.wait("bz", d, xi, 3)
-        if "a" in kinds:
-            for delta in GROUPS[t]:
-                for d in (0, 1):
-                    self.wait("ax", d, delta, 1)
+    def settle_a(self, t):
+        for delta in GROUPS[t]:
+            for d in (0, 1):
+                self.wait("ax", d, delta, 1)
+
+    def settle_b(self, u):
+        for xi in COLUMNS[u]:
+            for d in (0, 1):
+                self.wait("bz", d, xi, 3)
 
     def finish(self):
         for key, piece in self.started:
@@ -220,7 +220,7 @@
             tf[pl.ds(pl.multiple_of(c * 64, 64), 64), :] = row[:, 128 * n:128 * n + 128]
         return 0
 
-    lax.fori_loop(0, 96, mask_row, 0)
+    lax.fori_loop(0, 96, mask_row, 0, unroll=4)
     swap_copy(1 - y).wait_recv()
     gather.own(1)
 
@@ -253,21 +253,20 @@
             send_sem=t_send.at[d - 1, sb], recv_sem=t_recv.at[d - 1, sb],
             device_id=device(z, x, y, other), device_id_type=MESH)
 
-    for sb in range(4):
+    def hand_over(sb):
         lax.fori_loop(4 * sb, 4 * sb + 4, turn, 0)
         for d in range(1, NV):
             t_copy(d, sb).start()
+
     mine = pltpu.make_async_copy(
         u.at[:, :, pl.ds(pl.multiple_of(v * 96, 96), 96), :],
         s.at[:, pl.ds(0, 3), :, pl.ds(pl.multiple_of(v * 128, 128), 128)], one.at[0])
-    mine.start()
-
     pairs = ((0, 1), (7, 2), (6, 3), (5, 4))
 
     def zrow(delta):
         return pl.multiple_of(((z + delta) % NZ) * 128, 128)
 
-    def combine(g, _):
+    def combine_group(g, _):
         for blk in range(NV):
             lanes = pl.ds(128 * blk, 128)
             got = [s[g, m, :, lanes].astype(F32) for m in range(3)]
@@ -278,6 +277,11 @@
                 s[g, m, :, lanes] = (2.0 * straight - other).astype(BF16)
         return 0
 
+    def combine(sb):
+        for d in range(1, NV):
+            t_copy(d, sb, True).wait_recv()
+        lax.fori_loop(4 * sb, 4 * sb + 4, combine_group, 0)
+
     def pick(n):
         for delta in pairs[n]:
             rows = pl.ds(zrow(delta), 128)
@@ -293,20 +297,23 @@
             send_sem=f_send.at[d - 1, delta], recv_sem=f_recv.at[d - 1, delta],
             device_id=device(z, x, y, other), device_id_type=MESH)
 
-    def fit(n):
+    def fit(n, low, high):
         starts = [zrow(delta) for delta in pairs[n]]
+        total = acc.at[pl.ds(256 * n, 256), :]
 
         def step(kb, _):
             lanes = pl.ds(pl.multiple_of(kb * 768, 768), 768)
             left = jnp.concatenate([bg[pl.ds(a, 128), lanes] for a in starts], axis=0)
             part = jnp.dot(left, s[pl.ds(kb * 2, 2)].reshape(768, 512), preferred_element_type=F32)
-            acc[...] = jnp.where(kb == 0, 0.0, acc[...]) + part
+            total[...] = jnp.where(kb == 0, 0.0, total[...]) + part
             return 0
 
-        lax.fori_loop(0, 8, step, 0)
+        lax.fori_loop(2 * low, 2 * high, step, 0)
+
+    def reduce(n):
         for m, delta in enumerate(pairs[n]):
             rows = pl.ds(zrow(delta), 128)
-            turned = acc[pl.ds(128 * m, 128), :].T
+            turned = acc[pl.ds(256 * n + 128 * m, 128), :].T
             for blk in range(NV):
                 part = turned[128 * blk:128 * blk + 96]
                 fpart[blk, :, rows] = part.astype(BF16)
@@ -314,27 +321,41 @@
             for d in range(1, NV):
                 f_copy(d, delta, False).start()
 
+    hand_over(0)
     gather.wave(1)
+    hand_over(1)
     gather.wave(2)
+    hand_over(2)
+    hand_over(3)
+    mine.start()
     gather.wave(3)
-    gather.settle(0)
-    gather.settle(1)
+    gather.settle_a(0)
+    gather.settle_a(1)
     pick(0)
+    mine.wait()
+    combine(0)
+    combine(1)
+    fit(0, 0, 2)
     gather.wave(4)
-    gather.settle(2)
+    gather.settle_a(2)
     pick(1)
-    mine.wait()
-    for sb in range(4):
-        for d in range(1, NV):
-            t_copy(d, sb, True).wait_recv()
-    lax.fori_loop(0, 16, combine, 0)
-    fit(0)
+    combine(2)
+    fit(0, 2, 3)
+    fit(1, 0, 3)
     gather.wave(5)
-    fit(1)
-    gather.settle(3)
-    fit(2)
-    gather.settle(4)
-    fit(3)
+    combine(3)
+    fit(0, 3, 4)
+    reduce(0)
+    fit(1, 3, 4)
+    reduce(1)
+    gather.settle_a(3)
+    fit(2, 0, 4)
+    reduce(2)
+    gather.settle_a(4)
+    for column in range(3):
+        gather.settle_b(column)
+    fit(3, 0, 4)
+    reduce(3)
     pick(2)
     pick(3)
     two = pl.ds(pl.multiple_of((o % 4 - y) * 96, 96), 192)
@@ -407,65 +428,88 @@
         rows = pl.ds(pl.multiple_of(row, 32), size)
         r_v[rows, :] = (r_v[rows, :].astype(F32) + part).astype(BF16)
 
-    def r_copy(delta):
-        rows = pl.ds(pl.multiple_of(((z + delta) % NZ) * 256, 256), 256)
+    def spot(delta, xi):
+        return (z + delta) % NZ * NX + (x + xi) % NX
+
+    def r_copy(delta, xi):
+        rows = pl.ds(pl.multiple_of(spot(delta, xi) * 64, 64), 64)
         return pltpu.make_async_remote_copy(
-            src_ref=rsend.at[rows, :], dst_ref=rrecv.at[rows, :], send_sem=r_sem.at[delta],
-            recv_sem=rr_sem.at[delta], device_id=device(z, x, 1 - y, v), device_id_type=MESH)
-
-    def theirs(t):
+            src_ref=rsend.at[rows, :], dst_ref=rrecv.at[rows, :], send_sem=r_sem.at[delta * NX + xi],
+            recv_sem=rr_sem.at[delta * NX + xi], device_id=device(z, x, 1 - y, v), device_id_type=MESH)
+
+    def front(w):
+        return [(delta, xi) for u in range(3) for xi in COLUMNS[u] if 0 <= w - u <= 4 for delta in GROUPS[w - u]]
+
+    def early_rows(w):
+        return jnp.concatenate(
+            [fg[pl.ds(pl.multiple_of(spot(*at) * 128, 128), 64), :] for at in front(w)], axis=0)
+
+    def theirs(w):
+        part = jnp.dot(early_rows(w), second[...], preferred_element_type=F32).astype(BF16)
+        for n, at in enumerate(front(w)):
+            rsend[pl.ds(pl.multiple_of(spot(*at) * 64, 64), 64), :] = part[64 * n:64 * n + 64]
+            r_copy(*at).start()
+
+    def ours_early(w):
+        part = jnp.dot(early_rows(w), first[...], preferred_element_type=F32)
+        for n, at in enumerate(front(w)):
+            add((spot(*at) * NY + y) * 96, 64, part[64 * n:64 * n + 64])
+
+    def ours_late(t):
         for delta in GROUPS[t]:
-            zz = (z + delta) % NZ
             left = jnp.concatenate(
-                [fg[pl.ds(pl.multiple_of(zz * 512 + 128 * m, 128), 64), :] for m in range(NX)], axis=0)
-            part = jnp.dot(left, second[...], preferred_element_type=F32)
-            rsend[pl.ds(pl.multiple_of(zz * 256, 256), 256), :] = part.astype(BF16)
-            r_copy(delta).start()
-
-    def ours(t):
-        for delta in GROUPS[t]:
-            zz = (z + delta) % NZ
-            rows = pl.ds(pl.multiple_of(zz * 512, 512), 512)
-            part = jnp.dot(fg[rows, :], first[...], preferred_element_type=F32)
+                [fg[pl.ds(pl.multiple_of(spot(delta, m) * 128 + 64, 64), 64), :] for m in range(NX)], axis=0)
+            part = jnp.dot(left, first[...], preferred_element_type=F32)
             for m in range(NX):
-                pair = (zz * NX + m) * NY
-                add((pair + y) * 96, 96, part[128 * m:128 * m + 96])
-                add((pair + 1 - y) * 96 + 64, 32, part[128 * m + 96:128 * m + 128])
-
-    def arrived(t):
-        for delta in GROUPS[t]:
-            r_copy(delta).wait_recv()
-            zz = (z + delta) % NZ
-            for m in range(NX):
-                got = rrecv[pl.ds(pl.multiple_of(zz * 256 + 64 * m, 64), 64), :].astype(F32)
-                add(((zz * NX + m) * NY + 1 - y) * 96, 64, got)
-
+                pair = spot(delta, m) * NY
+                add((pair + y) * 96 + 64, 32, part[64 * m:64 * m + 32])
+                add((pair + 1 - y) * 96 + 64, 32, part[64 * m + 32:64 * m + 64])
+
+    def arrived(w):
+        for at in front(w):
+            r_copy(*at).wait_recv()
+            got = rrecv[pl.ds(pl.multiple_of(spot(*at) * 64, 64), 64), :].astype(F32)
+            add((spot(*at) * NY + 1 - y) * 96, 64, got)
+
+    theirs(0)
+    theirs(1)
     again.wave(2)
-    theirs(0)
+    theirs(2)
     share(*shares[1], 0, mate).wait_recv()
     share(*shares[1], 2, far).wait_recv()
     third[...] = wf[...].astype(F32).T.astype(BF16)
-    lax.fori_loop(0, 4, direct, 0)
+    lax.fori_loop(0, 8, direct, 0)
     again.wave(3)
-    theirs(1)
-    lax.fori_loop(4, 10, direct, 0)
+    theirs(3)
+    lax.fori_loop(8, 16, direct, 0)
+    for w in range(4):
+        ours_early(w)
     again.wave(4)
-    theirs(2)
-    lax.fori_loop(10, 16, direct, 0)
-    again.settle(0, "a")
-    ours(0)
-    again.settle(1, "a")
-    ours(1)
+    again.settle_b(0)
+    theirs(4)
+    ours_early(4)
+    for t in range(2):
+        again.settle_a(t)
+        ours_late(t)
+    for w in range(3):
+        arrived(w)
     again.wave(5)
-    theirs(3)
-    again.settle(4, "b")
-    theirs(4)
-    for t in range(2, 5):
-        again.settle(t, "a")
-        ours(t)
-        arrived(t - 2)
+    again.settle_b(1)
+    theirs(5)
+    ours_early(5)
+    again.settle_a(2)
+    ours_late(2)
     arrived(3)
+    again.settle_b(2)
+    theirs(6)
+    ours_early(6)
+    again.settle_a(3)
+    ours_late(3)
     arrived(4)
+    again.settle_a(4)
+    ours_late(4)
+    arrived(5)
+    arrived(6)
     save = pltpu.make_async_copy(r_v, r_hbm, one.at[0])
     save.start()
 
@@ -481,7 +525,8 @@
         for step in range(3):
             share(*share_args, step, across if step == 2 else v).wait_send()
     for delta in range(NZ):
-        r_copy(delta).wait_send()
+        for xi in range(NX):
+            r_copy(delta, xi).wait_send()
     again.finish()
     save.wait()
 
@@ -500,14 +545,14 @@
         scratch_shapes=[
             vmem((6144, 384), BF16), vmem((6144, 128), F32), vmem((6144, 128), F32), vmem((6144, 128), F32),
             vmem((6144, 512), BF16), vmem((16, 3, 384, 128), BF16), vmem((16, 4, 96, 512), BF16),
-            vmem((1024, 6144), BF16), vmem((256, 512), F32), vmem((NV, 96, 1024), BF16),
+            vmem((1024, 6144), BF16), vmem((1024, 512), F32), vmem((NV, 96, 1024), BF16),
             vmem((NV, 96, 1024), F32), vmem((NV, 96, 1024), BF16), vmem((384, 1024), BF16),
             vmem((64, 384), jnp.int32),
             vmem((4096, 1024), BF16), vmem((384, 1024), BF16), vmem((768, 1024), BF16),
             vmem((2048, 384), BF16), vmem((2048, 384), BF16),
             dma((N_SEMS,)), dma((N_SEMS,)), dma((N_SEMS,)), dma((N_SEMS,)),
             dma((3, 4)), dma((3, 4)), dma((3, 8)), dma((3, 8)),
-            dma((3,)), dma((3,)), dma((3,)), dma((3,)), dma((8,)), dma((8,)), dma((6,)),
+            dma((3,)), dma((3,)), dma((3,)), dma((3,)), dma((32,)), dma((32,)), dma((6,)),
         ],
         compiler_params=pltpu.CompilerParams(collective_id=0, has_side_effects=True, vmem_limit_bytes=63 << 20),
     )(amplitudes.reshape(6144, 384), jnp.transpose(aux_ints, (1, 2, 0)), occ_irrep, vir_irrep, vir_irrep[None, :])

time: 182 us -> 168 us (0.923)
  Pallas kernels: 173 us -> 159 us
    pallas_call x1, Pallas kernels: 173 us -> 159 us  [on_device(): pl.pallas_call(kernel, name='ccsd', out_shape=jax.ShapeDtypeStruct((6144,...]
where the time goes in v3:
time: 168 us; the launch traced here: 167 us
  Pallas kernels  159 us (95%)
  local copies, waits for them, and re-layouts  7.48 us (4%)
    pallas_call x1, Pallas kernels, on_device(): pl.pallas_call(kernel, name='ccsd', out_shape=jax.ShapeDtypeStruct((6144,...  159 us
    reshape x1, local copies, waits for them, and re-layouts, on_device(): return jnp.transpose(r.reshape(64, 96, 384), (1, 0, 2))[None]  6.24 us

profile of v3, /device:TPU:1, one launch (start us, length us, event | category | flops | bytes accessed | tf_op | source)
XLA Modules:
  0.0 166.9 jit_solution(6724025195736949551)
XLA Ops:
  0.0 1.2 broadcast_in_dim.6.vrow_ref
  1.2 159.4 %ccsd.1 = bf16[6144,384]{1,0:T(8,128)(2,1)} custom-call(bf16[6144,384]{1,0:T(8,128)(2,1)} %bitcast.9, bf16[64,16,96]{2,1,0:T(8,128)(2,1)} %bitcast.10, s32[64]{0:T(128)} %occ_ref.1, s32[384]{0:T(512)} %vir_ref.1, s32[1,384]{1,0:T(1,128)} %broadcast_in_dim.6.vrow_ref), custom_call_target="tpu_custom_call" | custom-call | tf_op jit(solution)/shard_map/ccsd/pallas_call | solution.py:539
  160.7 6.2 %copy.7 = bf16[64,96,384]{2,0,1:T(8,128)(2,1)} copy(bf16[64,96,384]{2,1,0:T(8,128)(2,1)} %bitcast.8) | data formatting | bytes 9437184 | tf_op jit(solution)/shard_map/reshape | solution.py:559

commit v4 on v3

--- a/solution.py
+++ b/solution.py
@@ -12,7 +12,7 @@
 BF16, F32 = jnp.bfloat16, jnp.float32
 GROUPS = ((0,), (1, 7), (2, 6), (3, 5), (4,))
 COLUMNS = ((0,), (1, 3), (2,))
-N_SEMS = 84
+N_SEMS = 100
 
 
 def position():
@@ -43,8 +43,8 @@
 
 
 class Gather:
-    def __init__(self, ref, block, region, two_pieces, send_sems, recv_sems):
-        self.ref, self.block, self.region, self.two_pieces = ref, block, region, two_pieces
+    def __init__(self, ref, block, region, two_pieces, far, send_sems, recv_sems):
+        self.ref, self.block, self.region, self.two_pieces, self.far = ref, block, region, two_pieces, far
         self.send_sems, self.recv_sems = send_sems, recv_sems
         self.z, self.x, self.y, self.v = position()
         self.started = []
@@ -57,11 +57,18 @@
             index = 8 + (d * 8 + key[2]) * 2 + key[3]
         elif kind == "bx":
             index = 40 + d * 2 + key[2]
+        elif kind == "bz":
+            index = 44 + (d * 4 + key[2]) * 4 + key[3]
         else:
-            index = 44 + (d * 4 + key[2]) * 4 + key[3]
+            index = 84 + d * 8 + key[2]
         if piece == 1:
             index = 76 + {"az": 0, "ax": 1, "bx": 2, "bz": 3}[kind] * 2 + d
-        (start, size), lanes = self.region(kind[0], half, piece)
+        if kind == "cx":
+            (start, size), lanes = (48 - 16 * d, 16), pl.ds(0, self.ref.shape[1])
+        elif self.far and kind == "bz" and key[2] == 2:
+            (start, size), lanes = (0, 32) if half is None else (16 * half, 16), pl.ds(0, self.ref.shape[1])
+        else:
+            (start, size), lanes = self.region(kind[0], half, piece)
         rows = pl.ds(pl.multiple_of((z % NZ * NX + x % NX) * self.block + start, 16), size)
         part = self.ref.at[rows, lanes]
         s = 1 - 2 * d
@@ -86,13 +93,15 @@
         elif kind == "bx":
             dz, dx = 0, -s * (key[2] + behind)
             half = d if key[2] == 1 else None
-        else:
+        elif kind == "bz":
             dz, dx = -s * (key[3] + behind), key[2]
             half = d if key[3] == 3 else None
+        else:
+            dz, dx = key[2], -s * (1 + behind)
         return self.z + dz + NZ, self.x + dx + NX, half
 
     def pieces(self, key):
-        own = key[2:] in ((0,), (0, 0))
+        own = key[0] != "cx" and key[2:] in ((0,), (0, 0))
         if not own:
             return (None,)
         return (0, 1) if key[0][0] in self.two_pieces else (0,)
@@ -148,6 +157,19 @@
                     for d in both:
                         self.wait("bz", d, xi, t)
                         self.send("bz", d, xi, t + 1)
+                if u == 1:
+                    self.send_far(t + 1)
+
+    def send_far(self, t):
+        if self.far:
+            for delta in GROUPS[t]:
+                for d in (0, 1):
+                    self.send("cx", d, delta)
+
+    def wait_far(self, t):
+        for delta in GROUPS[t]:
+            for d in (0, 1):
+                self.wait("cx", d, delta)
 
     def settle_a(self, t):
         for delta in GROUPS[t]:
@@ -158,6 +180,8 @@
         for xi in COLUMNS[u]:
             for d in (0, 1):
                 self.wait("bz", d, xi, 3)
+        if u == 1:
+            self.send_far(4)
 
     def finish(self):
         for key, piece in self.started:
@@ -200,11 +224,11 @@
         return rows, pl.ds(0, 3712) if kind == "a" else pl.ds(3712, 6144 - 3712)
 
     swap_copy(y).start()
-    gather = Gather(bg, 32, region, "ab", g_send, g_recv)
+    gather = Gather(bg, 32, region, "ab", False, g_send, g_recv)
     gather.own(0)
 
     mine_label = occ_ref[o]
-    vrow = vrow_ref[...]
+    vrow = vrow_ref[...].reshape(1, 384)
 
     def label_row(k, _):
         labels[pl.ds(k, 1), :] = vrow ^ (occ_ref[k] ^ mine_label)
@@ -282,6 +306,18 @@
             t_copy(d, sb, True).wait_recv()
         lax.fori_loop(4 * sb, 4 * sb + 4, combine_group, 0)
 
+    mate, across = v + 1 - 2 * (v % 2), (v + 2) % NV
+    far = (mate + 2) % NV
+    two = pl.ds(pl.multiple_of((o % 4 - y) * 96, 96), 192)
+
+    def share_v(step, delta, blk):
+        rows, lanes = pl.ds(pl.multiple_of(blk * 192, 192), 192), pl.ds(zrow(delta), 128)
+        into = bvf.at[rows, lanes]
+        return pltpu.make_async_remote_copy(
+            src_ref=into if step == 2 else bvt.at[two, lanes], dst_ref=into,
+            send_sem=v_send.at[step, delta], recv_sem=v_recv.at[step, delta],
+            device_id=device(z, x, y, across if step == 1 else mate), device_id_type=MESH)
+
     def pick(n):
         for delta in pairs[n]:
             rows = pl.ds(zrow(delta), 128)
@@ -297,7 +333,7 @@
             send_sem=f_send.at[d - 1, delta], recv_sem=f_recv.at[d - 1, delta],
             device_id=device(z, x, y, other), device_id_type=MESH)
 
-    def fit(n, low, high):
+    def fit(n, low, high, fresh=False):
         starts = [zrow(delta) for delta in pairs[n]]
         total = acc.at[pl.ds(256 * n, 256), :]
 
@@ -305,10 +341,10 @@
             lanes = pl.ds(pl.multiple_of(kb * 768, 768), 768)
             left = jnp.concatenate([bg[pl.ds(a, 128), lanes] for a in starts], axis=0)
             part = jnp.dot(left, s[pl.ds(kb * 2, 2)].reshape(768, 512), preferred_element_type=F32)
-            total[...] = jnp.where(kb == 0, 0.0, total[...]) + part
+            total[...] = (jnp.where(kb == low, 0.0, total[...]) if fresh else total[...]) + part
             return 0
 
-        lax.fori_loop(2 * low, 2 * high, step, 0)
+        lax.fori_loop(low, high, step, 0)
 
     def reduce(n):
         for m, delta in enumerate(pairs[n]):
@@ -335,30 +371,39 @@
     mine.wait()
     combine(0)
     combine(1)
-    fit(0, 0, 2)
+    fit(0, 0, 4, True)
     gather.wave(4)
     gather.settle_a(2)
     pick(1)
+    for n in range(2):
+        for delta in pairs[n]:
+            share_v(1, delta, v).start()
+            share_v(0, delta, v).start()
     combine(2)
-    fit(0, 2, 3)
-    fit(1, 0, 3)
+    fit(0, 4, 6)
+    fit(1, 0, 6, True)
     gather.wave(5)
     combine(3)
-    fit(0, 3, 4)
+    fit(0, 6, 8)
     reduce(0)
-    fit(1, 3, 4)
+    fit(1, 6, 8)
     reduce(1)
+    fit(2, 5, 8, True)
     gather.settle_a(3)
-    fit(2, 0, 4)
+    fit(2, 0, 5)
     reduce(2)
-    gather.settle_a(4)
     for column in range(3):
         gather.settle_b(column)
-    fit(3, 0, 4)
+    fit(3, 5, 8, True)
+    gather.settle_a(4)
+    fit(3, 0, 5)
     reduce(3)
     pick(2)
     pick(3)
-    two = pl.ds(pl.multiple_of((o % 4 - y) * 96, 96), 192)
+    for n in range(2):
+        for delta in pairs[n]:
+            share_v(1, delta, across).wait_recv()
+            share_v(2, delta, across).start()
     same = pltpu.make_async_copy(bvt.at[two, :], bvf.at[pl.ds(pl.multiple_of(v * 192, 192), 192), :], one.at[0])
     same.start()
 
@@ -378,13 +423,10 @@
         send_sem=one.at[4], recv_sem=one.at[5], device_id=device(z, x, 1 - y, v), device_id_type=MESH)
     swap.start()
 
-    mate, across = v + 1 - 2 * (v % 2), (v + 2) % NV
-    far = (mate + 2) % NV
-
-    def share(ref, size, send_sems, recv_sems, step, blk):
-        rows = pl.ds(pl.multiple_of(blk * size, size), size)
+    def share_w(step, blk):
+        rows = pl.ds(pl.multiple_of(blk * 96, 96), 96)
         return pltpu.make_async_remote_copy(
-            src_ref=ref.at[rows, :], dst_ref=ref.at[rows, :], send_sem=send_sems.at[step], recv_sem=recv_sems.at[step],
+            src_ref=wf.at[rows, :], dst_ref=wf.at[rows, :], send_sem=w_send.at[step], recv_sem=w_recv.at[step],
             device_id=device(z, x, y, across if step == 1 else mate), device_id_type=MESH)
 
     def region2(kind, half, piece):
@@ -396,22 +438,26 @@
             rows = (64, 64) if half is None else (64 + 32 * half, 32)
         return rows, pl.ds(0, 1024)
 
-    again = Gather(fg, 128, region2, "a", g2_send, g2_recv)
+    again = Gather(fg, 128, region2, "a", True, g2_send, g2_recv)
     again.own(0)
     same.wait()
-    shares = ((bvf, 192, v_send, v_recv), (wf, 96, w_send, w_recv))
-    for share_args in shares:
-        share(*share_args, 1, v).start()
-        share(*share_args, 0, v).start()
+    late = pairs[2] + pairs[3]
+    for delta in late:
+        share_v(1, delta, v).start()
+        share_v(0, delta, v).start()
+    share_w(1, v).start()
+    share_w(0, v).start()
     swap.wait_recv()
     again.own(1)
-    for share_args in shares:
-        share(*share_args, 1, across).wait_recv()
-        share(*share_args, 2, across).start()
-        if share_args is shares[0]:
-            again.wave(1)
-    share(*shares[0], 0, mate).wait_recv()
-    share(*shares[0], 2, far).wait_recv()
+    for delta in late:
+        share_v(1, delta, across).wait_recv()
+        share_v(2, delta, across).start()
+    again.wave(1)
+    share_w(1, across).wait_recv()
+    share_w(2, across).start()
+    for delta in range(NZ):
+        share_v(0, delta, mate).wait_recv()
+        share_v(2, delta, far).wait_recv()
     first, second, third = (cd.at[pl.ds(1024 * n, 1024), pl.ds(0, 384)] for n in range(3))
     for ref, which in ((second, 1 - y), (first, y)):
         whole = jnp.concatenate(
@@ -475,17 +521,19 @@
     theirs(1)
     again.wave(2)
     theirs(2)
-    share(*shares[1], 0, mate).wait_recv()
-    share(*shares[1], 2, far).wait_recv()
+    share_w(0, mate).wait_recv()
+    share_w(2, far).wait_recv()
     third[...] = wf[...].astype(F32).T.astype(BF16)
     lax.fori_loop(0, 8, direct, 0)
     again.wave(3)
+    again.wait_far(1)
     theirs(3)
     lax.fori_loop(8, 16, direct, 0)
     for w in range(4):
         ours_early(w)
     again.wave(4)
     again.settle_b(0)
+    again.wait_far(2)
     theirs(4)
     ours_early(4)
     for t in range(2):
@@ -495,12 +543,14 @@
         arrived(w)
     again.wave(5)
     again.settle_b(1)
+    again.wait_far(3)
     theirs(5)
     ours_early(5)
     again.settle_a(2)
     ours_late(2)
     arrived(3)
     again.settle_b(2)
+    again.wait_far(4)
     theirs(6)
     ours_early(6)
     again.settle_a(3)
@@ -521,9 +571,10 @@
     swap_copy(y).wait_send()
     gather.finish()
     swap.wait_send()
-    for share_args in shares:
-        for step in range(3):
-            share(*share_args, step, across if step == 2 else v).wait_send()
+    for step in range(3):
+        share_w(step, across if step == 2 else v).wait_send()
+        for delta in range(NZ):
+            share_v(step, delta, across if step == 2 else v).wait_send()
     for delta in range(NZ):
         for xi in range(NX):
             r_copy(delta, xi).wait_send()
@@ -552,10 +603,10 @@
             vmem((2048, 384), BF16), vmem((2048, 384), BF16),
             dma((N_SEMS,)), dma((N_SEMS,)), dma((N_SEMS,)), dma((N_SEMS,)),
             dma((3, 4)), dma((3, 4)), dma((3, 8)), dma((3, 8)),
-            dma((3,)), dma((3,)), dma((3,)), dma((3,)), dma((32,)), dma((32,)), dma((6,)),
+            dma((3,)), dma((3,)), dma((3, 8)), dma((3, 8)), dma((32,)), dma((32,)), dma((6,)),
         ],
         compiler_params=pltpu.CompilerParams(collective_id=0, has_side_effects=True, vmem_limit_bytes=63 << 20),
-    )(amplitudes.reshape(6144, 384), jnp.transpose(aux_ints, (1, 2, 0)), occ_irrep, vir_irrep, vir_irrep[None, :])
+    )(amplitudes.reshape(6144, 384), jnp.transpose(aux_ints, (1, 2, 0)), occ_irrep, vir_irrep, vir_irrep)
     return jnp.transpose(r.reshape(64, 96, 384), (1, 0, 2))[None]
 
 

time: 168 us -> 162 us (0.964); the launches traced: 167 us -> 159 us
  Pallas kernels: 159 us -> 152 us
    pallas_call x1, Pallas kernels: 159 us -> 152 us  [on_device(): pl.pallas_call(kernel, name='ccsd', out_shape=jax.ShapeDtypeStruct((6144,...]
where the time goes in v4:
time: 162 us; the launch traced here: 159 us
  Pallas kernels  152 us (94%)
  local copies, waits for them, and re-layouts  6.24 us (4%)
    pallas_call x1, Pallas kernels, on_device(): pl.pallas_call(kernel, name='ccsd', out_shape=jax.ShapeDtypeStruct((6144,...  152 us
    reshape x1, local copies, waits for them, and re-layouts, on_device(): return jnp.transpose(r.reshape(64, 96, 384), (1, 0, 2))[None]  6.24 us

profile of v4, /device:TPU:1, one launch (start us, length us, event | category | flops | bytes accessed | tf_op | source)
XLA Modules:
  0.0 158.5 jit_solution(5525144364214859059)
XLA Ops:
  0.0 152.3 %ccsd.1 = bf16[6144,384]{1,0:T(8,128)(2,1)} custom-call(bf16[6144,384]{1,0:T(8,128)(2,1)} %bitcast.9, bf16[64,16,96]{2,1,0:T(8,128)(2,1)} %bitcast.10, s32[64]{0:T(128)} %occ_ref.1, s32[384]{0:T(512)} %vrow_ref.1, s32[384]{0:T(512)} %vrow_ref.1), custom_call_target="tpu_custom_call" | custom-call | tf_op jit(solution)/shard_map/ccsd/pallas_call | solution.py:590
  152.3 6.2 %copy.7 = bf16[64,96,384]{2,0,1:T(8,128)(2,1)} copy(bf16[64,96,384]{2,1,0:T(8,128)(2,1)} %bitcast.8) | data formatting | bytes 9437184 | tf_op jit(solution)/shard_map/reshape | solution.py:610

commit v5 on v4

--- a/solution.py
+++ b/solution.py
@@ -43,8 +43,9 @@
 
 
 class Gather:
-    def __init__(self, ref, block, region, two_pieces, far, send_sems, recv_sems):
-        self.ref, self.block, self.region, self.two_pieces, self.far = ref, block, region, two_pieces, far
+    def __init__(self, ref, base, block, region, two_pieces, far, send_sems, recv_sems):
+        self.ref, self.base, self.block, self.region = ref, base, block, region
+        self.two_pieces, self.far = two_pieces, far
         self.send_sems, self.recv_sems = send_sems, recv_sems
         self.z, self.x, self.y, self.v = position()
         self.started = []
@@ -63,13 +64,12 @@
             index = 84 + d * 8 + key[2]
         if piece == 1:
             index = 76 + {"az": 0, "ax": 1, "bx": 2, "bz": 3}[kind] * 2 + d
+        (start, size), lanes = self.region("b" if kind == "cx" else kind[0], half, piece)
         if kind == "cx":
-            (start, size), lanes = (48 - 16 * d, 16), pl.ds(0, self.ref.shape[1])
+            start, size = 48 - 16 * d, 16
         elif self.far and kind == "bz" and key[2] == 2:
-            (start, size), lanes = (0, 32) if half is None else (16 * half, 16), pl.ds(0, self.ref.shape[1])
-        else:
-            (start, size), lanes = self.region(kind[0], half, piece)
-        rows = pl.ds(pl.multiple_of((z % NZ * NX + x % NX) * self.block + start, 16), size)
+            start, size = (0, 32) if half is None else (16 * half, 16)
+        rows = pl.ds(pl.multiple_of(self.base + (z % NZ * NX + x % NX) * self.block + start, 16), size)
         part = self.ref.at[rows, lanes]
         s = 1 - 2 * d
         if kind[1] == "z":
@@ -192,13 +192,14 @@
 def kernel(t_hbm, b_ref, occ_ref, vir_ref, vrow_ref, r_hbm,
            r_v, tf0, tf1, tf2, cd, u, s, bg, acc, fpart, fown, frecv, bvt, labels,
            fg, wf, bvf, rsend, rrecv,
-           g_send, g_recv, g2_send, g2_recv, t_send, t_recv, f_send, f_recv,
+           g_sems, t_send, t_recv, f_send, f_recv,
            w_send, w_recv, v_send, v_recv, r_sem, rr_sem, one):
     z, x, y, v = position()
     o = (z * NX + x) * NY + y
     load_t = pltpu.make_async_copy(t_hbm, r_v, one.at[0])
     load_t.start()
-    own = pl.ds(pl.multiple_of(o * 16, 16), 16)
+    here = (z * NX + x) * 16
+    own = pl.ds(pl.multiple_of(y * 512 + here, 16), 16)
 
     def place_b(n, _):
         four = jnp.concatenate([b_ref[4 * n + m].astype(F32) for m in range(4)], axis=1)
@@ -209,23 +210,20 @@
     barrier(peers_of(z, x, y, v))
 
     def swap_copy(there):
-        rows = pl.ds(pl.multiple_of((o - y + there) * 16, 16), 16)
+        rows = pl.ds(pl.multiple_of(there * 512 + here, 16), 16)
         return pltpu.make_async_remote_copy(
             src_ref=bg.at[rows, :], dst_ref=bg.at[rows, :], send_sem=one.at[2], recv_sem=one.at[3],
             device_id=device(z, x, 1 - y, v), device_id_type=MESH)
 
     def region(kind, half, piece):
-        if piece is not None:
-            rows = ((y if piece == 0 else 1 - y) * 16, 16)
-        elif half is not None:
-            rows = (half * 16, 16)
-        else:
-            rows = (0, 32)
-        return rows, pl.ds(0, 3712) if kind == "a" else pl.ds(3712, 6144 - 3712)
+        low, middle, high = (0, 1920, 3712) if kind == "a" else (3712, 4992, 6144)
+        low, high = (low, high) if half is None else ((low, middle), (middle, high))[half]
+        return (0, 16), pl.ds(low, high - low)
 
     swap_copy(y).start()
-    gather = Gather(bg, 32, region, "ab", False, g_send, g_recv)
-    gather.own(0)
+    near = Gather(bg, y * 512, 16, region, "", False, g_sems.at[0], g_sems.at[1])
+    other = Gather(bg, (1 - y) * 512, 16, region, "", False, g_sems.at[2], g_sems.at[3])
+    near.own(0)
 
     mine_label = occ_ref[o]
     vrow = vrow_ref[...].reshape(1, 384)
@@ -245,9 +243,6 @@
         return 0
 
     lax.fori_loop(0, 96, mask_row, 0, unroll=4)
-    swap_copy(1 - y).wait_recv()
-    gather.own(1)
-
     lane = lax.broadcasted_iota(jnp.int32, (96, 128), 1)
 
     def turn(g, _):
@@ -285,10 +280,8 @@
     mine = pltpu.make_async_copy(
         u.at[:, :, pl.ds(pl.multiple_of(v * 96, 96), 96), :],
         s.at[:, pl.ds(0, 3), :, pl.ds(pl.multiple_of(v * 128, 128), 128)], one.at[0])
-    pairs = ((0, 1), (7, 2), (6, 3), (5, 4))
-
-    def zrow(delta):
-        return pl.multiple_of(((z + delta) % NZ) * 128, 128)
+    def plane(which):
+        return pl.ds(pl.multiple_of(512 * (y if which == 0 else 1 - y), 512), 512)
 
     def combine_group(g, _):
         for blk in range(NV):
@@ -310,118 +303,156 @@
     far = (mate + 2) % NV
     two = pl.ds(pl.multiple_of((o % 4 - y) * 96, 96), 192)
 
-    def share_v(step, delta, blk):
-        rows, lanes = pl.ds(pl.multiple_of(blk * 192, 192), 192), pl.ds(zrow(delta), 128)
+    def share_v(step, which, blk):
+        rows, lanes = pl.ds(pl.multiple_of(blk * 192, 192), 192), plane(which)
         into = bvf.at[rows, lanes]
         return pltpu.make_async_remote_copy(
             src_ref=into if step == 2 else bvt.at[two, lanes], dst_ref=into,
-            send_sem=v_send.at[step, delta], recv_sem=v_recv.at[step, delta],
+            send_sem=v_send.at[step, which], recv_sem=v_recv.at[step, which],
             device_id=device(z, x, y, across if step == 1 else mate), device_id_type=MESH)
 
-    def pick(n):
-        for delta in pairs[n]:
-            rows = pl.ds(zrow(delta), 128)
-            four = bg[rows, pl.ds(pl.multiple_of((o // 4) * 384, 384), 384)]
-            bvt[:, rows] = four.astype(F32).T.astype(BF16)
-
-    def f_copy(d, delta, wait):
-        lanes = pl.ds(zrow(delta), 128)
-        other = (v + NV - d) % NV if wait else (v + d) % NV
-        here = other if wait else v
-        return pltpu.make_async_remote_copy(
-            src_ref=fpart.at[other, :, lanes], dst_ref=frecv.at[here, :, lanes],
-            send_sem=f_send.at[d - 1, delta], recv_sem=f_recv.at[d - 1, delta],
-            device_id=device(z, x, y, other), device_id_type=MESH)
-
-    def fit(n, low, high, fresh=False):
-        starts = [zrow(delta) for delta in pairs[n]]
-        total = acc.at[pl.ds(256 * n, 256), :]
-
+    def pick(which):
+        four = bg[plane(which), pl.ds(pl.multiple_of((o // 4) * 384, 384), 384)]
+        bvt[:, plane(which)] = four.astype(F32).T.astype(BF16)
+
+    def f_copy(d, which, wait):
+        lanes = plane(which)
+        peer = (v + NV - d) % NV if wait else (v + d) % NV
+        source = peer if wait else v
+        return pltpu.make_async_remote_copy(
+            src_ref=fpart.at[peer, :, lanes], dst_ref=frecv.at[source, :, lanes],
+            send_sem=f_send.at[d - 1, which], recv_sem=f_recv.at[d - 1, which],
+            device_id=device(z, x, y, peer), device_id_type=MESH)
+
+    def fit(parts, low, high, fresh=False):
         def step(kb, _):
             lanes = pl.ds(pl.multiple_of(kb * 768, 768), 768)
-            left = jnp.concatenate([bg[pl.ds(a, 128), lanes] for a in starts], axis=0)
+            left = [bg[pl.ds(pl.multiple_of(a, 64), size), lanes] for a, size in parts]
+            left = left[0] if len(left) == 1 else jnp.concatenate(left, axis=0)
             part = jnp.dot(left, s[pl.ds(kb * 2, 2)].reshape(768, 512), preferred_element_type=F32)
-            total[...] = (jnp.where(kb == low, 0.0, total[...]) if fresh else total[...]) + part
+            at = 0
+            for a, size in parts:
+                into = acc.at[pl.ds(pl.multiple_of(a, 64), size), :]
+                piece = part[at:at + size]
+                into[...] = (jnp.where(kb == low, 0.0, into[...]) if fresh else into[...]) + piece
+                at += size
             return 0
 
         lax.fori_loop(low, high, step, 0)
 
-    def reduce(n):
-        for m, delta in enumerate(pairs[n]):
-            rows = pl.ds(zrow(delta), 128)
-            turned = acc[pl.ds(256 * n + 128 * m, 128), :].T
+    def strips(deltas):
+        return [((1 - y) * 512 + (z + delta) % NZ * 64, 64) for delta in deltas]
+
+    whole = [(y * 512, 512)]
+
+    def reduce(which):
+        for m in range(4):
+            rows = pl.ds(pl.multiple_of(512 * (y if which == 0 else 1 - y) + 128 * m, 128), 128)
+            turned = acc[rows, :].T
             for blk in range(NV):
                 part = turned[128 * blk:128 * blk + 96]
                 fpart[blk, :, rows] = part.astype(BF16)
                 fown[blk, :, rows] = part
-            for d in range(1, NV):
-                f_copy(d, delta, False).start()
+        for d in range(1, NV):
+            f_copy(d, which, False).start()
+
+    block = pl.multiple_of((z * NX + x) * 128, 128)
+
+    def collect(which):
+        for d in range(1, NV):
+            f_copy(d, which, True).wait_recv()
+        lanes = plane(which)
+        total = fown[v, :, lanes]
+        for d in range(1, NV):
+            total = total + frecv[(v + NV - d) % NV, :, lanes].astype(F32)
+        total = total.astype(BF16)
+        fg[pl.ds(block, 96), lanes] = total
+        wf[pl.ds(pl.multiple_of(v * 96, 96), 96), lanes] = total
+
+    def e_copy(which, wait):
+        into = plane(1 - which)
+        return pltpu.make_async_remote_copy(
+            src_ref=fg.at[pl.ds(block + 64, 32), plane(which)], dst_ref=fg.at[pl.ds(block + 96, 32), plane(which) if wait else into],
+            send_sem=one.at[4 + which], recv_sem=one.at[6 + which],
+            device_id=device(z, x, 1 - y, v), device_id_type=MESH)
+
+    def region2(which):
+        def region(kind, half, piece):
+            if kind == "b":
+                rows = (0, 64) if half is None else (32 * half, 32)
+            elif piece is not None:
+                rows = (64 + 32 * piece, 32)
+            else:
+                rows = (64, 64) if half is None else (64 + 32 * half, 32)
+            return rows, plane(which)
+
+        return region
+
+    first_half = Gather(fg, 0, 128, region2(0), "a", True, g_sems.at[4], g_sems.at[5])
+    second_half = Gather(fg, 0, 128, region2(1), "a", True, g_sems.at[6], g_sems.at[7])
 
     hand_over(0)
-    gather.wave(1)
+    near.wave(1)
     hand_over(1)
-    gather.wave(2)
+    near.wave(2)
     hand_over(2)
     hand_over(3)
     mine.start()
-    gather.wave(3)
-    gather.settle_a(0)
-    gather.settle_a(1)
+    near.wave(3)
+    swap_copy(1 - y).wait_recv()
+    other.own(0)
+    near.wave(4)
+    near.wave(5)
+    for n in range(3):
+        near.settle_b(n)
+    for n in range(5):
+        near.settle_a(n)
     pick(0)
+    share_v(1, 0, v).start()
+    share_v(0, 0, v).start()
+    other.wave(1)
     mine.wait()
     combine(0)
     combine(1)
-    fit(0, 0, 4, True)
-    gather.wave(4)
-    gather.settle_a(2)
+    other.wave(2)
+    fit(whole, 0, 4, True)
+    other.wave(3)
+    combine(2)
+    fit(whole, 4, 6)
+    other.wave(4)
+    combine(3)
+    fit(whole, 6, 8)
+    reduce(0)
+    other.wave(5)
+    for n in range(2):
+        other.settle_a(n)
+    fit(strips((0, 1, 7)), 0, 8, True)
+    collect(0)
+    e_copy(0, False).start()
+    first_half.own(0)
+    other.settle_a(2)
+    fit(strips((2, 6)), 0, 8, True)
+    share_v(1, 0, across).wait_recv()
+    share_v(2, 0, across).start()
+    e_copy(0, True).wait_recv()
+    first_half.own(1)
+    for n in range(3):
+        other.settle_b(n)
+    fit(strips((3, 5, 4)), 5, 8, True)
+    first_half.wave(1)
+    for n in range(3, 5):
+        other.settle_a(n)
+    fit(strips((3, 5, 4)), 0, 5)
+    reduce(1)
     pick(1)
-    for n in range(2):
-        for delta in pairs[n]:
-            share_v(1, delta, v).start()
-            share_v(0, delta, v).start()
-    combine(2)
-    fit(0, 4, 6)
-    fit(1, 0, 6, True)
-    gather.wave(5)
-    combine(3)
-    fit(0, 6, 8)
-    reduce(0)
-    fit(1, 6, 8)
-    reduce(1)
-    fit(2, 5, 8, True)
-    gather.settle_a(3)
-    fit(2, 0, 5)
-    reduce(2)
-    for column in range(3):
-        gather.settle_b(column)
-    fit(3, 5, 8, True)
-    gather.settle_a(4)
-    fit(3, 0, 5)
-    reduce(3)
-    pick(2)
-    pick(3)
-    for n in range(2):
-        for delta in pairs[n]:
-            share_v(1, delta, across).wait_recv()
-            share_v(2, delta, across).start()
     same = pltpu.make_async_copy(bvt.at[two, :], bvf.at[pl.ds(pl.multiple_of(v * 192, 192), 192), :], one.at[0])
     same.start()
-
-    for d in range(1, NV):
-        for delta in range(NZ):
-            f_copy(d, delta, True).wait_recv()
-    total = fown[v]
-    for d in range(1, NV):
-        total = total + frecv[(v + NV - d) % NV].astype(F32)
-    total = total.astype(BF16)
-    block = pl.multiple_of((z * NX + x) * 128, 128)
-    fg[pl.ds(block, 96), :] = total
-    wf[pl.ds(pl.multiple_of(v * 96, 96), 96), :] = total
-
-    swap = pltpu.make_async_remote_copy(
-        src_ref=fg.at[pl.ds(block + 64, 32), :], dst_ref=fg.at[pl.ds(block + 96, 32), :],
-        send_sem=one.at[4], recv_sem=one.at[5], device_id=device(z, x, 1 - y, v), device_id_type=MESH)
-    swap.start()
+    first_half.wave(2)
+    collect(1)
+    e_copy(1, False).start()
+    second_half.own(0)
+    share_v(1, 1, v).start()
+    share_v(0, 1, v).start()
 
     def share_w(step, blk):
         rows = pl.ds(pl.multiple_of(blk * 96, 96), 96)
@@ -429,40 +460,27 @@
             src_ref=wf.at[rows, :], dst_ref=wf.at[rows, :], send_sem=w_send.at[step], recv_sem=w_recv.at[step],
             device_id=device(z, x, y, across if step == 1 else mate), device_id_type=MESH)
 
-    def region2(kind, half, piece):
-        if kind == "b":
-            rows = (0, 64) if half is None else (32 * half, 32)
-        elif piece is not None:
-            rows = (64 + 32 * piece, 32)
-        else:
-            rows = (64, 64) if half is None else (64 + 32 * half, 32)
-        return rows, pl.ds(0, 1024)
-
-    again = Gather(fg, 128, region2, "a", True, g2_send, g2_recv)
-    again.own(0)
-    same.wait()
-    late = pairs[2] + pairs[3]
-    for delta in late:
-        share_v(1, delta, v).start()
-        share_v(0, delta, v).start()
     share_w(1, v).start()
     share_w(0, v).start()
-    swap.wait_recv()
-    again.own(1)
-    for delta in late:
-        share_v(1, delta, across).wait_recv()
-        share_v(2, delta, across).start()
-    again.wave(1)
+    first_half.wave(3)
+    e_copy(1, True).wait_recv()
+    second_half.own(1)
+    share_v(1, 1, across).wait_recv()
+    share_v(2, 1, across).start()
+    second_half.wave(1)
     share_w(1, across).wait_recv()
     share_w(2, across).start()
-    for delta in range(NZ):
-        share_v(0, delta, mate).wait_recv()
-        share_v(2, delta, far).wait_recv()
-    first, second, third = (cd.at[pl.ds(1024 * n, 1024), pl.ds(0, 384)] for n in range(3))
+    same.wait()
+    for which in range(2):
+        share_v(0, which, mate).wait_recv()
+        share_v(2, which, far).wait_recv()
+    first, second, third, turned = (cd.at[pl.ds(1024 * n, 1024), pl.ds(0, 384)] for n in range(4))
     for ref, which in ((second, 1 - y), (first, y)):
-        whole = jnp.concatenate(
+        wide = jnp.concatenate(
             [bvf[pl.ds(pl.multiple_of(blk * 192 + which * 96, 96), 96), :] for blk in range(NV)], axis=0)
-        ref[...] = whole.astype(F32).T.astype(BF16)
+        ref[...] = wide.astype(F32).T.astype(BF16)
+    turned[pl.ds(0, 512), :] = first[pl.ds(512, 512), :]
+    turned[pl.ds(512, 512), :] = first[pl.ds(0, 512), :]
 
     def direct(n, _):
         lanes = pl.ds(pl.multiple_of(n * 384, 384), 384)
@@ -503,13 +521,12 @@
 
     def ours_late(t):
         for delta in GROUPS[t]:
-            left = jnp.concatenate(
-                [fg[pl.ds(pl.multiple_of(spot(delta, m) * 128 + 64, 64), 64), :] for m in range(NX)], axis=0)
-            part = jnp.dot(left, first[...], preferred_element_type=F32)
-            for m in range(NX):
-                pair = spot(delta, m) * NY
-                add((pair + y) * 96 + 64, 32, part[64 * m:64 * m + 32])
-                add((pair + 1 - y) * 96 + 64, 32, part[64 * m + 32:64 * m + 64])
+            for start, weights, row in ((64, first, y * 96 + 64), (96, turned, (1 - y) * 96 + 64)):
+                left = jnp.concatenate(
+                    [fg[pl.ds(pl.multiple_of(spot(delta, m) * 128 + start, 32), 32), :] for m in range(NX)], axis=0)
+                part = jnp.dot(left, weights[...], preferred_element_type=F32)
+                for m in range(NX):
+                    add(spot(delta, m) * NY * 96 + row, 32, part[32 * m:32 * m + 32])
 
     def arrived(w):
         for at in front(w):
@@ -519,44 +536,55 @@
 
     theirs(0)
     theirs(1)
-    again.wave(2)
+    first_half.wave(4)
+    first_half.settle_b(0)
+    second_half.wave(2)
     theirs(2)
     share_w(0, mate).wait_recv()
     share_w(2, far).wait_recv()
     third[...] = wf[...].astype(F32).T.astype(BF16)
+    first_half.wave(5)
+    first_half.settle_b(1)
     lax.fori_loop(0, 8, direct, 0)
-    again.wave(3)
-    again.wait_far(1)
+    second_half.wave(3)
+    first_half.wait_far(1)
+    second_half.wait_far(1)
     theirs(3)
     lax.fori_loop(8, 16, direct, 0)
     for w in range(4):
         ours_early(w)
-    again.wave(4)
-    again.settle_b(0)
-    again.wait_far(2)
+    second_half.wave(4)
+    second_half.settle_b(0)
+    first_half.wait_far(2)
+    second_half.wait_far(2)
     theirs(4)
     ours_early(4)
+    first_half.settle_b(2)
+    first_half.wait_far(3)
+    first_half.wait_far(4)
+    for t in range(5):
+        first_half.settle_a(t)
     for t in range(2):
-        again.settle_a(t)
+        second_half.settle_a(t)
         ours_late(t)
     for w in range(3):
         arrived(w)
-    again.wave(5)
-    again.settle_b(1)
-    again.wait_far(3)
+    second_half.wave(5)
+    second_half.settle_b(1)
+    second_half.wait_far(3)
     theirs(5)
     ours_early(5)
-    again.settle_a(2)
+    second_half.settle_a(2)
     ours_late(2)
     arrived(3)
-    again.settle_b(2)
-    again.wait_far(4)
+    second_half.settle_b(2)
+    second_half.wait_far(4)
     theirs(6)
     ours_early(6)
-    again.settle_a(3)
+    second_half.settle_a(3)
     ours_late(3)
     arrived(4)
-    again.settle_a(4)
+    second_half.settle_a(4)
     ours_late(4)
     arrived(5)
     arrived(6)
@@ -564,21 +592,22 @@
     save.start()
 
     for d in range(1, NV):
-        for delta in range(NZ):
-            f_copy(d, delta, False).wait_send()
+        for which in range(2):
+            f_copy(d, which, False).wait_send()
         for sb in range(4):
             t_copy(d, sb).wait_send()
     swap_copy(y).wait_send()
-    gather.finish()
-    swap.wait_send()
     for step in range(3):
         share_w(step, across if step == 2 else v).wait_send()
-        for delta in range(NZ):
-            share_v(step, delta, across if step == 2 else v).wait_send()
+        for which in range(2):
+            share_v(step, which, across if step == 2 else v).wait_send()
+    for which in range(2):
+        e_copy(which, False).wait_send()
     for delta in range(NZ):
         for xi in range(NX):
             r_copy(delta, xi).wait_send()
-    again.finish()
+    for ring in (near, other, first_half, second_half):
+        ring.finish()
     save.wait()
 
 
@@ -601,9 +630,9 @@
             vmem((64, 384), jnp.int32),
             vmem((4096, 1024), BF16), vmem((384, 1024), BF16), vmem((768, 1024), BF16),
             vmem((2048, 384), BF16), vmem((2048, 384), BF16),
-            dma((N_SEMS,)), dma((N_SEMS,)), dma((N_SEMS,)), dma((N_SEMS,)),
-            dma((3, 4)), dma((3, 4)), dma((3, 8)), dma((3, 8)),
-            dma((3,)), dma((3,)), dma((3, 8)), dma((3, 8)), dma((32,)), dma((32,)), dma((6,)),
+            dma((8, N_SEMS)),
+            dma((3, 4)), dma((3, 4)), dma((3, 2)), dma((3, 2)),
+            dma((3,)), dma((3,)), dma((3, 2)), dma((3, 2)), dma((32,)), dma((32,)), dma((8,)),
         ],
         compiler_params=pltpu.CompilerParams(collective_id=0, has_side_effects=True, vmem_limit_bytes=63 << 20),
     )(amplitudes.reshape(6144, 384), jnp.transpose(aux_ints, (1, 2, 0)), occ_irrep, vir_irrep, vir_irrep)

time: 162 us -> 166 us (1.025)
  Pallas kernels: 152 us -> 157 us
    pallas_call x1, Pallas kernels: 152 us -> 157 us  [on_device(): pl.pallas_call(kernel, name='ccsd', out_shape=jax.ShapeDtypeStruct((6144,...]
where the time goes in v5:
time: 166 us; the launch traced here: 163 us
  Pallas kernels  157 us (95%)
  local copies, waits for them, and re-layouts  6.24 us (4%)
    pallas_call x1, Pallas kernels, on_device(): pl.pallas_call(kernel, name='ccsd', out_shape=jax.ShapeDtypeStruct((6144,...  157 us
    reshape x1, local copies, waits for them, and re-layouts, on_device(): return jnp.transpose(r.reshape(64, 96, 384), (1, 0, 2))[None]  6.24 us

profile of v5, /device:TPU:1, one launch (start us, length us, event | category | flops | bytes accessed | tf_op | source)
XLA Modules:
  0.0 163.2 jit_solution(10131012633648033002)
XLA Ops:
  0.0 157.0 %ccsd.1 = bf16[6144,384]{1,0:T(8,128)(2,1)} custom-call(bf16[6144,384]{1,0:T(8,128)(2,1)} %bitcast.9, bf16[64,16,96]{2,1,0:T(8,128)(2,1)} %bitcast.10, s32[64]{0:T(128)} %occ_ref.1, s32[384]{0:T(512)} %vrow_ref.1, s32[384]{0:T(512)} %vrow_ref.1), custom_call_target="tpu_custom_call" | custom-call | tf_op jit(solution)/shard_map/ccsd/pallas_call | solution.py:619
  157.0 6.2 %copy.7 = bf16[64,96,384]{2,0,1:T(8,128)(2,1)} copy(bf16[64,96,384]{2,1,0:T(8,128)(2,1)} %bitcast.8) | data formatting | bytes 9437184 | tf_op jit(solution)/shard_map/reshape | solution.py:639

commit v6 on v4

--- a/solution.py
+++ b/solution.py
@@ -17,7 +17,7 @@
 
 def position():
     o, v = lax.axis_index("occ"), lax.axis_index("vir")
-    return o // (NX * NY), (o // NY) % NX, o % NY, v
+    return o >> 3, (o >> 1) & (NX - 1), o & (NY - 1), v
 
 
 def device(z, x, y, v):
@@ -39,14 +39,20 @@
         device(z, (x + NX - 1) % NX, y, v),
         device(z, x, 1 - y, v),
     ]
-    return ring + [device(z, x, y, (v + d) % NV) for d in range(1, NV)]
+    return ring + [device(z, x, y, (v + d) & (NV - 1)) for d in range(1, NV)]
 
 
 class Gather:
     def __init__(self, ref, block, region, two_pieces, far, send_sems, recv_sems):
         self.ref, self.block, self.region, self.two_pieces, self.far = ref, block, region, two_pieces, far
         self.send_sems, self.recv_sems = send_sems, recv_sems
-        self.z, self.x, self.y, self.v = position()
+        z, x, y, v = position()
+        self.z_rows = [((z + n) & (NZ - 1)) * (NX * block) for n in range(NZ)]
+        self.x_rows = [((x + n) & (NX - 1)) * block for n in range(NX)]
+        self.targets = {
+            "z": [device((z + n) & (NZ - 1), x, y, v) for n in (1, NZ - 1)],
+            "x": [device(z, (x + n) & (NX - 1), y, v) for n in (1, NX - 1)],
+        }
         self.started = []
 
     def copy(self, key, z, x, half, piece):
@@ -69,13 +75,9 @@
             (start, size), lanes = (0, 32) if half is None else (16 * half, 16), pl.ds(0, self.ref.shape[1])
         else:
             (start, size), lanes = self.region(kind[0], half, piece)
-        rows = pl.ds(pl.multiple_of((z % NZ * NX + x % NX) * self.block + start, 16), size)
+        rows = pl.ds(pl.multiple_of(self.z_rows[z % NZ] + self.x_rows[x % NX] + start, 16), size)
         part = self.ref.at[rows, lanes]
-        s = 1 - 2 * d
-        if kind[1] == "z":
-            target = device((self.z + s + NZ) % NZ, self.x, self.y, self.v)
-        else:
-            target = device(self.z, (self.x + s + NX) % NX, self.y, self.v)
+        target = self.targets[kind[1]][d]
         return pltpu.make_async_remote_copy(
             src_ref=part, dst_ref=part, send_sem=self.send_sems.at[index],
             recv_sem=self.recv_sems.at[index], device_id=target, device_id_type=MESH)
@@ -98,7 +100,7 @@
             half = d if key[3] == 3 else None
         else:
             dz, dx = key[2], -s * (1 + behind)
-        return self.z + dz + NZ, self.x + dx + NX, half
+        return dz, dx, half
 
     def pieces(self, key):
         own = key[0] != "cx" and key[2:] in ((0,), (0, 0))
@@ -193,7 +195,7 @@
            r_v, tf0, tf1, tf2, cd, u, s, bg, acc, fpart, fown, frecv, bvt, labels,
            fg, wf, bvf, rsend, rrecv,
            g_send, g_recv, g2_send, g2_recv, t_send, t_recv, f_send, f_recv,
-           w_send, w_recv, v_send, v_recv, r_sem, rr_sem, one):
+           w_send, w_recv, v_send, v_recv, r_sem, rr_sem, out_sem, one):
     z, x, y, v = position()
     o = (z * NX + x) * NY + y
     load_t = pltpu.make_async_copy(t_hbm, r_v, one.at[0])
@@ -237,16 +239,18 @@
     lax.fori_loop(0, 64, label_row, 0)
     load_t.wait()
 
-    def mask_row(c, _):
-        row = r_v[pl.ds(pl.multiple_of(c * 64, 64), 64), :].astype(F32)
-        row = jnp.where(labels[...] == vir_ref[v * 96 + c], row, 0.0)
-        for n, tf in enumerate((tf0, tf1, tf2)):
-            tf[pl.ds(pl.multiple_of(c * 64, 64), 64), :] = row[:, 128 * n:128 * n + 128]
-        return 0
-
-    lax.fori_loop(0, 96, mask_row, 0, unroll=4)
-    swap_copy(1 - y).wait_recv()
-    gather.own(1)
+    def mask(sb):
+        wanted = labels[pl.ds(16 * sb, 16), :]
+
+        def mask_row(c, _):
+            rows = pl.ds(pl.multiple_of(c * 64 + 16 * sb, 16), 16)
+            row = jnp.where(wanted == vir_ref[v * 96 + c], r_v[rows, :].astype(F32), 0.0)
+            for n, tf in enumerate((tf0, tf1, tf2)):
+                tf[rows, :] = row[:, 128 * n:128 * n + 128]
+            return 0
+
+        lax.fori_loop(0, 96, mask_row, 0, unroll=8)
+
 
     lane = lax.broadcasted_iota(jnp.int32, (96, 128), 1)
 
@@ -269,7 +273,7 @@
         return 0
 
     def t_copy(d, sb, wait=False):
-        other = (v + NV - d) % NV if wait else (v + d) % NV
+        other = (v + NV - d) & (NV - 1) if wait else (v + d) & (NV - 1)
         here = other if wait else v
         return pltpu.make_async_remote_copy(
             src_ref=u.at[pl.ds(4 * sb, 4), :, pl.ds(pl.multiple_of(other * 96, 96), 96), :],
@@ -278,6 +282,7 @@
             device_id=device(z, x, y, other), device_id_type=MESH)
 
     def hand_over(sb):
+        mask(sb)
         lax.fori_loop(4 * sb, 4 * sb + 4, turn, 0)
         for d in range(1, NV):
             t_copy(d, sb).start()
@@ -288,7 +293,7 @@
     pairs = ((0, 1), (7, 2), (6, 3), (5, 4))
 
     def zrow(delta):
-        return pl.multiple_of(((z + delta) % NZ) * 128, 128)
+        return pl.multiple_of((((z + delta) & (NZ - 1))) * 128, 128)
 
     def combine_group(g, _):
         for blk in range(NV):
@@ -306,8 +311,8 @@
             t_copy(d, sb, True).wait_recv()
         lax.fori_loop(4 * sb, 4 * sb + 4, combine_group, 0)
 
-    mate, across = v + 1 - 2 * (v % 2), (v + 2) % NV
-    far = (mate + 2) % NV
+    mate, across = v + 1 - 2 * (v % 2), (v + 2) & (NV - 1)
+    far = (mate + 2) & (NV - 1)
     two = pl.ds(pl.multiple_of((o % 4 - y) * 96, 96), 192)
 
     def share_v(step, delta, blk):
@@ -326,7 +331,7 @@
 
     def f_copy(d, delta, wait):
         lanes = pl.ds(zrow(delta), 128)
-        other = (v + NV - d) % NV if wait else (v + d) % NV
+        other = (v + NV - d) & (NV - 1) if wait else (v + d) & (NV - 1)
         here = other if wait else v
         return pltpu.make_async_remote_copy(
             src_ref=fpart.at[other, :, lanes], dst_ref=frecv.at[here, :, lanes],
@@ -358,6 +363,8 @@
                 f_copy(d, delta, False).start()
 
     hand_over(0)
+    swap_copy(1 - y).wait_recv()
+    gather.own(1)
     gather.wave(1)
     hand_over(1)
     gather.wave(2)
@@ -412,7 +419,7 @@
             f_copy(d, delta, True).wait_recv()
     total = fown[v]
     for d in range(1, NV):
-        total = total + frecv[(v + NV - d) % NV].astype(F32)
+        total = total + frecv[(v + NV - d) & (NV - 1)].astype(F32)
     total = total.astype(BF16)
     block = pl.multiple_of((z * NX + x) * 128, 128)
     fg[pl.ds(block, 96), :] = total
@@ -475,7 +482,7 @@
         r_v[rows, :] = (r_v[rows, :].astype(F32) + part).astype(BF16)
 
     def spot(delta, xi):
-        return (z + delta) % NZ * NX + (x + xi) % NX
+        return ((z + delta) & (NZ - 1)) * NX + ((x + xi) & (NX - 1))
 
     def r_copy(delta, xi):
         rows = pl.ds(pl.multiple_of(spot(delta, xi) * 64, 64), 64)
@@ -516,6 +523,14 @@
             r_copy(*at).wait_recv()
             got = rrecv[pl.ds(pl.multiple_of(spot(*at) * 64, 64), 64), :].astype(F32)
             add((spot(*at) * NY + 1 - y) * 96, 64, got)
+
+    def save_copy(delta):
+        rows = pl.ds(pl.multiple_of(((z + delta) & (NZ - 1)) * 768, 768), 768)
+        return pltpu.make_async_copy(r_v.at[rows, :], r_hbm.at[rows, :], out_sem.at[delta])
+
+    def save(t):
+        for delta in GROUPS[t]:
+            save_copy(delta).start()
 
     theirs(0)
     theirs(1)
@@ -541,6 +556,7 @@
         ours_late(t)
     for w in range(3):
         arrived(w)
+    save(0)
     again.wave(5)
     again.settle_b(1)
     again.wait_far(3)
@@ -549,6 +565,7 @@
     again.settle_a(2)
     ours_late(2)
     arrived(3)
+    save(1)
     again.settle_b(2)
     again.wait_far(4)
     theirs(6)
@@ -556,12 +573,13 @@
     again.settle_a(3)
     ours_late(3)
     arrived(4)
+    save(2)
     again.settle_a(4)
     ours_late(4)
     arrived(5)
+    save(3)
     arrived(6)
-    save = pltpu.make_async_copy(r_v, r_hbm, one.at[0])
-    save.start()
+    save(4)
 
     for d in range(1, NV):
         for delta in range(NZ):
@@ -579,7 +597,8 @@
         for xi in range(NX):
             r_copy(delta, xi).wait_send()
     again.finish()
-    save.wait()
+    for delta in range(NZ):
+        save_copy(delta).wait()
 
 
 def on_device(amplitudes, aux_ints, occ_irrep, vir_irrep):
@@ -603,7 +622,7 @@
             vmem((2048, 384), BF16), vmem((2048, 384), BF16),
             dma((N_SEMS,)), dma((N_SEMS,)), dma((N_SEMS,)), dma((N_SEMS,)),
             dma((3, 4)), dma((3, 4)), dma((3, 8)), dma((3, 8)),
-            dma((3,)), dma((3,)), dma((3, 8)), dma((3, 8)), dma((32,)), dma((32,)), dma((6,)),
+            dma((3,)), dma((3,)), dma((3, 8)), dma((3, 8)), dma((32,)), dma((32,)), dma((8,)), dma((6,)),
         ],
         compiler_params=pltpu.CompilerParams(collective_id=0, has_side_effects=True, vmem_limit_bytes=63 << 20),
     )(amplitudes.reshape(6144, 384), jnp.transpose(aux_ints, (1, 2, 0)), occ_irrep, vir_irrep, vir_irrep)

time: 162 us -> 161 us (level)
  no operation moved by 1% of the time
where the time goes in v6:
time: 161 us; the launch traced here: 159 us
  Pallas kernels  153 us (95%)
  local copies, waits for them, and re-layouts  6.24 us (4%)
    pallas_call x1, Pallas kernels, on_device(): pl.pallas_call(kernel, name='ccsd', out_shape=jax.ShapeDtypeStruct((6144,...  153 us
    reshape x1, local copies, waits for them, and re-layouts, on_device(): return jnp.transpose(r.reshape(64, 96, 384), (1, 0, 2))[None]  6.24 us

profile of v6, /device:TPU:1, one launch (start us, length us, event | category | flops | bytes accessed | tf_op | source)
XLA Modules:
  0.0 159.0 jit_solution(10917636220809996826)
XLA Ops:
  0.0 152.8 %ccsd.1 = bf16[6144,384]{1,0:T(8,128)(2,1)} custom-call(bf16[6144,384]{1,0:T(8,128)(2,1)} %bitcast.9, bf16[64,16,96]{2,1,0:T(8,128)(2,1)} %bitcast.10, s32[64]{0:T(128)} %occ_ref.1, s32[384]{0:T(512)} %vrow_ref.1, s32[384]{0:T(512)} %vrow_ref.1), custom_call_target="tpu_custom_call" | custom-call | tf_op jit(solution)/shard_map/ccsd/pallas_call | solution.py:609
  152.8 6.2 %copy.7 = bf16[64,96,384]{2,0,1:T(8,128)(2,1)} copy(bf16[64,96,384]{2,1,0:T(8,128)(2,1)} %bitcast.8) | data formatting | bytes 9437184 | tf_op jit(solution)/shard_map/reshape | solution.py:629
